TPU v7x, 128 devices: a whole 4x4x4 slice. The times are simulated.
128 devices in a mesh: tok: 2 (over y_hi), fin: 16 (over z, x), fout: 4 (over y_lo, core).
Axes of the slice: x: 4, y: 4 (y_hi: 2, y_lo: 2; y = y_hi * 2 + y_lo), z: 4, core: 2. Of those that a mesh axis runs over, the one named last changes fastest.
Arguments:
- tokens: bfloat16 [1024, 6144], P(('tok', 'fout'), 'fin'), may hold values from -6 to 6
- out_grad: bfloat16 [1024, 6144], P(('tok', 'fout'), 'fin'), may hold values from -3 to 3
- up_weight: bfloat16 [6144, 24576], P(('fin', 'tok'), 'fout'), may hold values from -0.078125 to 0.078125
- down_weight: bfloat16 [6144, 24576], P(('fin', 'tok'), 'fout'), may hold values from -0.0390625 to 0.0390625
Outputs:
- grad_tokens: bfloat16 [1024, 6144], P(('tok', 'fout'), 'fin')
- grad_up: float32 [6144, 24576], P(('fin', 'tok'), 'fout')
- grad_down: float32 [6144, 24576], P(('fin', 'tok'), 'fout')
All inputs are finite; a program needn't handle non-finite values.
Results may differ from a plain program's by a relative error of at most 0.025.
Values may be sent and summed in bfloat16 or wider, within the bound.
No kernel may reach another device: no remote copies, remote signals or barrier semaphores. Data moves between devices by JAX's collectives and lax.ppermute only.
A program may use at most 128 MiB of HBM per device.

v0:
```python
import jax
import jax.numpy as jnp
from jax import lax
from jax.sharding import Mesh
from jax.sharding import PartitionSpec as P

AXES = ("yh", "z", "x", "yl", "c")
CHUNKS = 2
SWAP = [(0, 1), (1, 0)]


def ring(step, along_x):
    pairs = []
    for z in range(4):
        for x in range(4):
            for c in range(2):
                to = (z, (x + step) % 4) if (c == 0) == along_x else ((z + step) % 4, x)
                pairs.append(((z * 4 + x) * 2 + c, (to[0] * 4 + to[1]) * 2 + c))
    return pairs


def deal(value, step):
    return lax.ppermute(value, ("z", "x", "c"), ring(step, True))


def pass_on(value, step):
    return lax.ppermute(value, ("z", "x", "c"), ring(step, False))


def swap(value, axis):
    return lax.ppermute(value, axis, SWAP)


def ordered(first, mine, other, axis):
    return jnp.where(
        first, jnp.concatenate([mine, other], axis), jnp.concatenate([other, mine], axis)
    )


def pick(value, index):
    return lax.dynamic_index_in_dim(value, index, 0, keepdims=False)


def halves(value, index, axis):
    half = value.shape[axis] // 2
    return (
        lax.dynamic_slice_in_dim(value, index * half, half, axis),
        lax.dynamic_slice_in_dim(value, (1 - index) * half, half, axis),
    )


def activate(preact, grad_act):
    activation, pullback = jax.vjp(lambda value: jax.nn.gelu(value, approximate=True), preact)
    grad_pre = pullback(grad_act)[0]
    return (activation.astype(jnp.bfloat16), grad_pre.astype(jnp.bfloat16))


def gather_tokens(tokens, out_grad, tok, yl, core):
    turned = jnp.stack([tokens.T, out_grad.T])
    held, other = halves(turned, tok, 1)
    held = ordered(tok == 0, held, swap(other, "yh"), 2)
    held = ordered(yl == 0, held, swap(held, "yl"), 2)
    held = ordered(core == 0, held, swap(held, "c"), 2)
    parts = [held] + [deal(held, k) for k in (1, 2, 3)]
    return [jnp.concatenate([p[i] for p in parts], 0) for i in range(2)]


def spread(up, down, start, width, place):
    got = []
    for k in range(4):
        at = start + lax.rem(place + k, 4) * width
        piece = jnp.concatenate(
            [lax.dynamic_slice_in_dim(w, at, width, 1) for w in (up, down)], 0
        )
        got.append(piece if k == 0 else deal(piece, k))
    rows = up.shape[0]
    return (
        jnp.concatenate([g[:rows] for g in got], 0),
        jnp.concatenate([g[rows:] for g in got], 0),
    )


def scatter_sum(pre, act, place, tok):
    f32 = jnp.float32
    bf16 = jnp.bfloat16
    pre = pre.reshape(4, pre.shape[0] // 4, -1)
    act = act.reshape(pre.shape)
    after, across, before = (lax.rem(place + k, 4) for k in (1, 2, 3))
    pre_in = pass_on(pick(pre, across), 1)
    act_in = pass_on(pick(act, across), -1)
    to_after = jnp.stack([(pick(pre, after).astype(f32) + pre_in.astype(f32)).astype(bf16), pick(act, after)])
    to_before = jnp.stack([pick(pre, before), (pick(act, before).astype(f32) + act_in.astype(f32)).astype(bf16)])
    from_before = pass_on(to_after, 1)
    from_after = pass_on(to_before, -1)
    own = jnp.stack([pick(pre, place), pick(act, place)])
    total = own.astype(f32) + from_before.astype(f32) + from_after.astype(f32)
    mine, other = halves(total, tok, 1)
    return mine + swap(other.astype(bf16), "yh").astype(f32)


def gather_rows(activation, grad_pre, place, tok):
    mine = jnp.stack([activation, grad_pre])
    pair = ordered(tok == 0, mine, swap(mine, "yh"), 1)
    from_before = pass_on(pair, 1)
    from_after = pass_on(pair, -1)
    activ_across = pass_on(from_before[0], 1)
    grad_across = pass_on(from_after[1], -1)
    after, across, before = (lax.rem(place + k, 4) for k in (1, 2, 3))
    outs = []
    for own, prev, later, far in (
        (pair[0], from_before[0], from_after[0], activ_across),
        (pair[1], from_before[1], from_after[1], grad_across),
    ):
        full = jnp.zeros((4,) + own.shape, own.dtype)
        for at, block in ((place, own), (before, prev), (after, later), (across, far)):
            full = lax.dynamic_update_slice(full, block[None], (at, 0, 0))
        outs.append(full.reshape(-1, own.shape[1]))
    return outs


def local(tokens, out_grad, up, down):
    f32 = jnp.float32
    bf16 = jnp.bfloat16
    tok, yl, core = lax.axis_index("yh"), lax.axis_index("yl"), lax.axis_index("c")
    x, z = lax.axis_index("x"), lax.axis_index("z")
    dealt = jnp.where(core == 0, x, z)
    summed = jnp.where(core == 0, z, x)
    rows = up.shape[0]
    width = up.shape[1] // (4 * CHUNKS)
    first = (((0,), (0,)), ((), ()))
    last = (((1,), (1,)), ((), ()))
    plain = (((1,), (0,)), ((), ()))

    def mul(a, b, dims):
        return lax.dot_general(a, b, dims, preferred_element_type=f32).astype(bf16)

    weights = [spread(up, down, j * 4 * width, width, dealt) for j in range(CHUNKS)]
    x_cols, g_cols = gather_tokens(tokens, out_grad, tok, yl, core)
    shares = []
    for j in range(CHUNKS):
        pre = mul(x_cols, weights[j][0], first)
        act = mul(g_cols, weights[j][1], first)
        sums = scatter_sum(pre, act, summed, tok)
        shares.append(activate(sums[0], sums[1]))
    part = 0
    grads = []
    for j in range(CHUNKS):
        activation, grad_pre = gather_rows(*shares[j], summed, tok)
        part = part + lax.dot_general(weights[j][0], grad_pre, last, preferred_element_type=f32)
        grads.append((mul(x_cols, grad_pre, plain), mul(g_cols, activation, plain)))
    held = part.astype(bf16)
    total = part[:rows]
    for k in (1, 2, 3):
        total = total + deal(held[k * rows : (k + 1) * rows], -k).astype(f32)
    for axis, at in (("c", core), ("yl", yl)):
        mine, other = halves(total, at, 1)
        total = mine + swap(other.astype(bf16), axis).astype(f32)
    mine, other = halves(total.astype(bf16), tok, 1)
    grad_tokens = ordered(tok == 0, mine, swap(other, "yh"), 0).T

    grad_up = jnp.zeros(up.shape, f32)
    grad_down = jnp.zeros(up.shape, f32)
    for j in range(CHUNKS):
        for k in range(4):
            piece = jnp.concatenate([g[k * rows : (k + 1) * rows] for g in grads[j]], 0)
            if k:
                piece = deal(piece, -k)
            at = j * 4 * width + lax.rem(dealt + k, 4) * width
            grad_up = lax.dynamic_update_slice(grad_up, piece[:rows].astype(f32), (0, at))
            grad_down = lax.dynamic_update_slice(grad_down, piece[rows:].astype(f32), (0, at))
    return (grad_tokens, grad_up, grad_down)


def solution(mesh):
    cube = Mesh(mesh.devices.reshape(2, 4, 4, 2, 2), AXES)
    rows = P(("yh", "yl", "c"), ("z", "x"))
    weight = P(("z", "x", "yh"), ("yl", "c"))
    return jax.shard_map(
        local,
        mesh=cube,
        in_specs=(rows, rows, weight, weight),
        out_specs=(rows, weight, weight),
        check_vma=False,
    )
```

profile of v0, /device:TPU:0, one launch (start us, length us, event | category | flops | bytes accessed | tf_op | source)
XLA Modules:
  0.0 214.5 jit_solution(9577295921352975493)
XLA Ops:
  0.7 3.5 %constant_dynamic-slice_fusion.17 = (bf16[192,768]{1,0:T(8,128)(2,1)}, bf16[192,768]{1,0:T(8,128)(2,1)S(1)}, bf16[192,768]{1,0:T(8,128)(2,1)S(1)}, bf16[192,768]...) fusion(bf16[192,6144]{1,0:T(8,128)(2,1)} %param.7, ...), kind=kLoop, calls=%fused_computation.169 | loop fusion | bytes 9437216 | tf_op jit(solution)/shard_map/dynamic_slice | solution.py:73
  20.4 4.4 %collective-permute-done.4 = bf16[2,192,256]{2,1,0:T(8,128)(2,1)S(1)} collective-permute-done((bf16[2,192,256]{2,1,0:T(8,128)(2,1)S(1)}, bf16[2,192,256]{2,1,0:T(8,128)(2,1)S(1)}, u32[]{:S(2)}, u32[]{:S(2)}) %collective-permute-start.4) | collective-permute-done | bytes 196640 | tf_op jit(solution)/shard_map/ppermute | solution.py:31
  24.8 3.7 %collective-permute-start.1 = (bf16[384,768]{1,0:T(8,128)(2,1)S(1)}, bf16[384,768]{1,0:T(8,128)(2,1)S(1)}, u32[]{:S(2)}, u32[]{:S(2)}) collective-permute-start(bf16[384,768]{1,0:T(8,128)(2,1)S(1)} %pad_maximum_fusion.9), channel_id=1, source_target_pairs={{0,8},{1,33},{4,12},{5,37},{8,0},{9,41},{12,4},{13,45},{16,24},{17... | collective-permute-start | bytes 1769480 | tf_op jit(solution)/shard_map/ppermute | solution.py:23
  31.8 3.3 %collective-permute-start.8 = (bf16[2,192,1024]{2,1,0:T(8,128)(2,1)S(1)}, bf16[2,192,1024]{2,1,0:T(8,128)(2,1)S(1)}, u32[]{:S(2)}, u32[]{:S(2)}) collective-permute-start(bf16[2,192,1024]{2,1,0:T(8,128)(2,1)S(1)} %maximum_select_fusion), channel_id=1, source_target_pairs={{0,12},{1,49},{4,0},{5,53},{8,4},{9,57},{12,8},{13,61},{16,28},{17... | collective-permute-start | bytes 2359304 | tf_op jit(solution)/shard_map/ppermute | solution.py:23
  37.9 4.8 %collective-permute-done = bf16[384,768]{1,0:T(8,128)(2,1)S(1)} collective-permute-done((bf16[384,768]{1,0:T(8,128)(2,1)S(1)}, bf16[384,768]{1,0:T(8,128)(2,1)S(1)}, u32[]{:S(2)}, u32[]{:S(2)}) %collective-permute-start) | collective-permute-done | bytes 589856 | tf_op jit(solution)/shard_map/ppermute | solution.py:23
  42.8 10.3 %collective-permute-done.8 = bf16[2,192,1024]{2,1,0:T(8,128)(2,1)S(1)} collective-permute-done((bf16[2,192,1024]{2,1,0:T(8,128)(2,1)S(1)}, bf16[2,192,1024]{2,1,0:T(8,128)(2,1)S(1)}, u32[]{:S(2)}, u32[]{:S(2)}) %collective-permute-start.8) | collective-permute-done | bytes 786464 | tf_op jit(solution)/shard_map/ppermute | solution.py:23
  53.2 6.3 %collective-permute-done.6 = bf16[2,192,1024]{2,1,0:T(8,128)(2,1)S(1)} collective-permute-done((bf16[2,192,1024]{2,1,0:T(8,128)(2,1)S(1)}, bf16[2,192,1024]{2,1,0:T(8,128)(2,1)S(1)}, u32[]{:S(2)}, u32[]{:S(2)}) %collective-permute-start.6) | collective-permute-done | bytes 786464 | tf_op jit(solution)/shard_map/ppermute | solution.py:23
  61.2 3.6 %collective-permute-start.23 = (bf16[256,768]{1,0:T(8,128)(2,1)S(1)}, bf16[256,768]{1,0:T(8,128)(2,1)S(1)}, u32[]{:S(2)}, u32[]{:S(2)}) collective-permute-start(bf16[256,768]{1,0:T(8,128)(2,1)S(1)} %get-tuple-element.38), channel_id=1, source_target_pairs={{0,48},{1,13},{4,52},{5,1},{8,56},{9,5},{12,60},{13,9},{16,0},{17,... | collective-permute-start | bytes 1179656 | tf_op jit(solution)/shard_map/ppermute | solution.py:27
  74.2 3.2 %collective-permute-start.24 = (bf16[2,256,768]{2,1,0:T(8,128)(2,1)}, bf16[2,256,768]{2,1,0:T(8,128)(2,1)}, u32[]{:S(2)}, u32[]{:S(2)}) collective-permute-start(bf16[2,256,768]{2,1,0:T(8,128)(2,1)} %pad_maximum_fusion.7), channel_id=1, source_target_pairs={{0,48},{1,13},{4,52},{5,1},{8,56},{9,5},{12,60},{13,9},{16,0},{17,... | collective-permute-start | bytes 2359304 | tf_op jit(solution)/shard_map/ppermute | solution.py:27
  79.5 3.2 %collective-permute-start.12 = (bf16[2,256,768]{2,1,0:T(8,128)(2,1)}, bf16[2,256,768]{2,1,0:T(8,128)(2,1)}, u32[]{:S(2)}, u32[]{:S(2)}) collective-permute-start(bf16[2,256,768]{2,1,0:T(8,128)(2,1)} %pad_maximum_fusion.5), channel_id=1, source_target_pairs={{0,48},{1,13},{4,52},{5,1},{8,56},{9,5},{12,60},{13,9},{16,0},{17,... | collective-permute-start | bytes 2359304 | tf_op jit(solution)/shard_map/ppermute | solution.py:27
  83.8 3.4 %collective-permute-done.24 = bf16[2,256,768]{2,1,0:T(8,128)(2,1)} collective-permute-done((bf16[2,256,768]{2,1,0:T(8,128)(2,1)}, bf16[2,256,768]{2,1,0:T(8,128)(2,1)}, u32[]{:S(2)}, u32[]{:S(2)}) %collective-permute-start.24) | collective-permute-done | bytes 786464 | tf_op jit(solution)/shard_map/ppermute | solution.py:27
  87.2 4.8 %collective-permute-done.22 = bf16[2,256,768]{2,1,0:T(8,128)(2,1)} collective-permute-done((bf16[2,256,768]{2,1,0:T(8,128)(2,1)}, bf16[2,256,768]{2,1,0:T(8,128)(2,1)}, u32[]{:S(2)}, u32[]{:S(2)}) %collective-permute-start.22) | collective-permute-done | bytes 786464 | tf_op jit(solution)/shard_map/ppermute | solution.py:27
  93.7 3.4 %collective-permute-start.25 = (bf16[2,128,768]{2,1,0:T(8,128)(2,1)S(1)}, bf16[2,128,768]{2,1,0:T(8,128)(2,1)S(1)}, u32[]{:S(2)}, u32[]{:S(2)}) collective-permute-start(bf16[2,128,768]{2,1,0:T(8,128)(2,1)S(1)} %dynamic-slice_convert_fusion), channel_id=1, source_target_pairs={{0,64},{64,0},{1,65},{65,1},{2,66},{66,2},{3,67},{67,3},{4,68},{68... | collective-permute-start | bytes 1179656 | tf_op jit(solution)/shard_map/ppermute | solution.py:31
  97.0 3.4 %collective-permute-done.10 = bf16[2,256,768]{2,1,0:T(8,128)(2,1)} collective-permute-done((bf16[2,256,768]{2,1,0:T(8,128)(2,1)}, bf16[2,256,768]{2,1,0:T(8,128)(2,1)}, u32[]{:S(2)}, u32[]{:S(2)}) %collective-permute-start.10) | collective-permute-done | bytes 786464 | tf_op jit(solution)/shard_map/ppermute | solution.py:27
  102.1 3.4 %collective-permute-start.13 = (bf16[2,128,768]{2,1,0:T(8,128)(2,1)S(1)}, bf16[2,128,768]{2,1,0:T(8,128)(2,1)S(1)}, u32[]{:S(2)}, u32[]{:S(2)}) collective-permute-start(bf16[2,128,768]{2,1,0:T(8,128)(2,1)S(1)} %dynamic-slice_convert_fusion.1), channel_id=1, source_target_pairs={{0,64},{64,0},{1,65},{65,1},{2,66},{66,2},{3,67},{67,3},{4,68},{68... | collective-permute-start | bytes 1179656 | tf_op jit(solution)/shard_map/ppermute | solution.py:31
  109.0 6.8 %collective-permute-done.13 = bf16[2,128,768]{2,1,0:T(8,128)(2,1)S(1)} collective-permute-done((bf16[2,128,768]{2,1,0:T(8,128)(2,1)S(1)}, bf16[2,128,768]{2,1,0:T(8,128)(2,1)S(1)}, u32[]{:S(2)}, u32[]{:S(2)}) %collective-permute-start.13) | collective-permute-done | bytes 393248 | tf_op jit(solution)/shard_map/ppermute | solution.py:31
  116.1 3.4 %collective-permute-start.14 = (bf16[2,128,768]{2,1,0:T(8,128)(2,1)S(1)}, bf16[2,128,768]{2,1,0:T(8,128)(2,1)}, u32[]{:S(2)}, u32[]{:S(2)}) collective-permute-start(bf16[2,128,768]{2,1,0:T(8,128)(2,1)S(1)} %pad_maximum_fusion.20), channel_id=1, source_target_pairs={{0,64},{64,0},{1,65},{65,1},{2,66},{66,2},{3,67},{67,3},{4,68},{68... | collective-permute-start | bytes 1179656 | tf_op jit(solution)/shard_map/ppermute | solution.py:31
  119.5 4.6 %collective-permute-done.26 = bf16[2,128,768]{2,1,0:T(8,128)(2,1)S(1)} collective-permute-done((bf16[2,128,768]{2,1,0:T(8,128)(2,1)S(1)}, bf16[2,128,768]{2,1,0:T(8,128)(2,1)S(1)}, u32[]{:S(2)}, u32[]{:S(2)}) %collective-permute-start.26) | collective-permute-done | bytes 393248 | tf_op jit(solution)/shard_map/ppermute | solution.py:31
  124.5 3.2 %collective-permute-start.28 = (bf16[2,256,768]{2,1,0:T(8,128)(2,1)S(1)}, bf16[2,256,768]{2,1,0:T(8,128)(2,1)S(1)}, u32[]{:S(2)}, u32[]{:S(2)}) collective-permute-start(bf16[2,256,768]{2,1,0:T(8,128)(2,1)S(1)} %maximum_select_fusion.2), channel_id=1, source_target_pairs={{0,48},{1,13},{4,52},{5,1},{8,56},{9,5},{12,60},{13,9},{16,0},{17,... | collective-permute-start | bytes 2359304 | tf_op jit(solution)/shard_map/ppermute | solution.py:27
  129.8 3.2 %collective-permute-start.16 = (bf16[2,256,768]{2,1,0:T(8,128)(2,1)S(1)}, bf16[2,256,768]{2,1,0:T(8,128)(2,1)S(1)}, u32[]{:S(2)}, u32[]{:S(2)}) collective-permute-start(bf16[2,256,768]{2,1,0:T(8,128)(2,1)S(1)} %maximum_select_fusion.1), channel_id=1, source_target_pairs={{0,48},{1,13},{4,52},{5,1},{8,56},{9,5},{12,60},{13,9},{16,0},{17,... | collective-permute-start | bytes 2359304 | tf_op jit(solution)/shard_map/ppermute | solution.py:27
  133.6 4.0 %collective-permute-done.27 = bf16[2,256,768]{2,1,0:T(8,128)(2,1)S(1)} collective-permute-done((bf16[2,256,768]{2,1,0:T(8,128)(2,1)S(1)}, bf16[2,256,768]{2,1,0:T(8,128)(2,1)S(1)}, u32[]{:S(2)}, u32[]{:S(2)}) %collective-permute-start.27) | collective-permute-done | bytes 786464 | tf_op jit(solution)/shard_map/ppermute | solution.py:27
  141.1 5.0 %collective-permute-done.15 = bf16[2,256,768]{2,1,0:T(8,128)(2,1)S(1)} collective-permute-done((bf16[2,256,768]{2,1,0:T(8,128)(2,1)S(1)}, bf16[2,256,768]{2,1,0:T(8,128)(2,1)S(1)}, u32[]{:S(2)}, u32[]{:S(2)}) %collective-permute-start.15) | collective-permute-done | bytes 786464 | tf_op jit(solution)/shard_map/ppermute | solution.py:27
  151.3 11.8 %collective-permute-done.17 = bf16[256,768]{1,0:T(8,128)(2,1)S(1)} collective-permute-done((bf16[256,768]{1,0:T(8,128)(2,1)S(1)}, bf16[256,768]{1,0:T(8,128)(2,1)S(1)}, u32[]{:S(2)}, u32[]{:S(2)}) %collective-permute-start.17) | collective-permute-done | bytes 393248 | tf_op jit(solution)/shard_map/ppermute | solution.py:27
  193.6 5.1 %collective-permute-done.39 = bf16[384,768]{1,0:T(8,128)(2,1)S(1)} collective-permute-done((bf16[384,768]{1,0:T(8,128)(2,1)S(1)}, bf16[384,768]{1,0:T(8,128)(2,1)S(1)}, u32[]{:S(2)}, u32[]{:S(2)}) %collective-permute-start.39) | collective-permute-done | bytes 589856 | tf_op jit(solution)/shard_map/ppermute | solution.py:23
  (224 shorter events, 101.1 us)
Async XLA Ops:
  5.0 23.5 %collective-permute-start.20 = (bf16[384,768]{1,0:T(8,128)(2,1)}, bf16[384,768]{1,0:T(8,128)(2,1)}, u32[]{:S(2)}, u32[]{:S(2)}) collective-permute-start(bf16[384,768]{1,0:T(8,128)(2,1)} %pad_maximum_fusion.13), channel_id=1, source_target_pairs={{0,12},{1,49},{4,0},{5,53},{8,4},{9,57},{12,8},{13,61},{16,28},{17... | collective-permute-start | bytes 1769480 | tf_op jit(solution)/shard_map/ppermute | solution.py:23
  8.7 21.0 %collective-permute-start.19 = (bf16[384,768]{1,0:T(8,128)(2,1)}, bf16[384,768]{1,0:T(8,128)(2,1)S(1)}, u32[]{:S(2)}, u32[]{:S(2)}) collective-permute-start(bf16[384,768]{1,0:T(8,128)(2,1)} %pad_maximum_fusion.12), channel_id=1, source_target_pairs={{0,8},{1,33},{4,12},{5,37},{8,0},{9,41},{12,4},{13,45},{16,24},{17... | collective-permute-start | bytes 1769480 | tf_op jit(solution)/shard_map/ppermute | solution.py:23
  10.4 19.5 %collective-permute-start.18 = (bf16[384,768]{1,0:T(8,128)(2,1)}, bf16[384,768]{1,0:T(8,128)(2,1)S(1)}, u32[]{:S(2)}, u32[]{:S(2)}) collective-permute-start(bf16[384,768]{1,0:T(8,128)(2,1)} %pad_maximum_fusion.11), channel_id=1, source_target_pairs={{0,4},{1,17},{4,8},{5,21},{8,12},{9,25},{12,0},{13,29},{16,20},{17... | collective-permute-start | bytes 1769480 | tf_op jit(solution)/shard_map/ppermute | solution.py:23
  16.3 18.8 %collective-permute-start.2 = (bf16[384,768]{1,0:T(8,128)(2,1)}, bf16[384,768]{1,0:T(8,128)(2,1)}, u32[]{:S(2)}, u32[]{:S(2)}) collective-permute-start(bf16[384,768]{1,0:T(8,128)(2,1)} %pad_maximum_fusion.10), channel_id=1, source_target_pairs={{0,12},{1,49},{4,0},{5,53},{8,4},{9,57},{12,8},{13,61},{16,28},{17... | collective-permute-start | bytes 1769480 | tf_op jit(solution)/shard_map/ppermute | solution.py:23
  28.6 14.1 %collective-permute-start = (bf16[384,768]{1,0:T(8,128)(2,1)S(1)}, bf16[384,768]{1,0:T(8,128)(2,1)S(1)}, u32[]{:S(2)}, u32[]{:S(2)}) collective-permute-start(bf16[384,768]{1,0:T(8,128)(2,1)S(1)} %pad_maximum_fusion.8), channel_id=1, source_target_pairs={{0,4},{1,17},{4,8},{5,21},{8,12},{9,25},{12,0},{13,29},{16,20},{17... | collective-permute-start | bytes 1769480 | tf_op jit(solution)/shard_map/ppermute | solution.py:23
  31.8 21.2 %collective-permute-start.8 = (bf16[2,192,1024]{2,1,0:T(8,128)(2,1)S(1)}, bf16[2,192,1024]{2,1,0:T(8,128)(2,1)S(1)}, u32[]{:S(2)}, u32[]{:S(2)}) collective-permute-start(bf16[2,192,1024]{2,1,0:T(8,128)(2,1)S(1)} %maximum_select_fusion), channel_id=1, source_target_pairs={{0,12},{1,49},{4,0},{5,53},{8,4},{9,57},{12,8},{13,61},{16,28},{17... | collective-permute-start | bytes 2359304 | tf_op jit(solution)/shard_map/ppermute | solution.py:23
  36.2 17.0 %collective-permute-start.7 = (bf16[2,192,1024]{2,1,0:T(8,128)(2,1)S(1)}, bf16[2,192,1024]{2,1,0:T(8,128)(2,1)S(1)}, u32[]{:S(2)}, u32[]{:S(2)}) collective-permute-start(bf16[2,192,1024]{2,1,0:T(8,128)(2,1)S(1)} %maximum_select_fusion), channel_id=1, source_target_pairs={{0,8},{1,33},{4,12},{5,37},{8,0},{9,41},{12,4},{13,45},{16,24},{17... | collective-permute-start | bytes 2359304 | tf_op jit(solution)/shard_map/ppermute | solution.py:23
  36.5 23.0 %collective-permute-start.6 = (bf16[2,192,1024]{2,1,0:T(8,128)(2,1)S(1)}, bf16[2,192,1024]{2,1,0:T(8,128)(2,1)S(1)}, u32[]{:S(2)}, u32[]{:S(2)}) collective-permute-start(bf16[2,192,1024]{2,1,0:T(8,128)(2,1)S(1)} %maximum_select_fusion), channel_id=1, source_target_pairs={{0,4},{1,17},{4,8},{5,21},{8,12},{9,25},{12,0},{13,29},{16,20},{17... | collective-permute-start | bytes 2359304 | tf_op jit(solution)/shard_map/ppermute | solution.py:23
  79.5 17.5 %collective-permute-start.12 = (bf16[2,256,768]{2,1,0:T(8,128)(2,1)}, bf16[2,256,768]{2,1,0:T(8,128)(2,1)}, u32[]{:S(2)}, u32[]{:S(2)}) collective-permute-start(bf16[2,256,768]{2,1,0:T(8,128)(2,1)} %pad_maximum_fusion.5), channel_id=1, source_target_pairs={{0,48},{1,13},{4,52},{5,1},{8,56},{9,5},{12,60},{13,9},{16,0},{17,... | collective-permute-start | bytes 2359304 | tf_op jit(solution)/shard_map/ppermute | solution.py:27
  83.8 16.6 %collective-permute-start.10 = (bf16[2,256,768]{2,1,0:T(8,128)(2,1)}, bf16[2,256,768]{2,1,0:T(8,128)(2,1)}, u32[]{:S(2)}, u32[]{:S(2)}) collective-permute-start(bf16[2,256,768]{2,1,0:T(8,128)(2,1)} %pad_maximum_fusion.4), channel_id=1, source_target_pairs={{0,16},{1,5},{4,20},{5,9},{8,24},{9,13},{12,28},{13,1},{16,32},{17... | collective-permute-start | bytes 2359304 | tf_op jit(solution)/shard_map/ppermute | solution.py:27
  105.9 18.2 %collective-permute-start.26 = (bf16[2,128,768]{2,1,0:T(8,128)(2,1)S(1)}, bf16[2,128,768]{2,1,0:T(8,128)(2,1)S(1)}, u32[]{:S(2)}, u32[]{:S(2)}) collective-permute-start(bf16[2,128,768]{2,1,0:T(8,128)(2,1)S(1)} %pad_maximum_fusion.21), channel_id=1, source_target_pairs={{0,64},{64,0},{1,65},{65,1},{2,66},{66,2},{3,67},{67,3},{4,68},{68... | collective-permute-start | bytes 1179656 | tf_op jit(solution)/shard_map/ppermute | solution.py:31
  129.7 16.4 %collective-permute-start.15 = (bf16[2,256,768]{2,1,0:T(8,128)(2,1)S(1)}, bf16[2,256,768]{2,1,0:T(8,128)(2,1)S(1)}, u32[]{:S(2)}, u32[]{:S(2)}) collective-permute-start(bf16[2,256,768]{2,1,0:T(8,128)(2,1)S(1)} %maximum_select_fusion.1), channel_id=1, source_target_pairs={{0,16},{1,5},{4,20},{5,9},{8,24},{9,13},{12,28},{13,1},{16,32},{17... | collective-permute-start | bytes 2359304 | tf_op jit(solution)/shard_map/ppermute | solution.py:27
  129.8 16.4 %collective-permute-start.16 = (bf16[2,256,768]{2,1,0:T(8,128)(2,1)S(1)}, bf16[2,256,768]{2,1,0:T(8,128)(2,1)S(1)}, u32[]{:S(2)}, u32[]{:S(2)}) collective-permute-start(bf16[2,256,768]{2,1,0:T(8,128)(2,1)S(1)} %maximum_select_fusion.1), channel_id=1, source_target_pairs={{0,48},{1,13},{4,52},{5,1},{8,56},{9,5},{12,60},{13,9},{16,0},{17,... | collective-permute-start | bytes 2359304 | tf_op jit(solution)/shard_map/ppermute | solution.py:27
  146.3 16.8 %collective-permute-start.17 = (bf16[256,768]{1,0:T(8,128)(2,1)S(1)}, bf16[256,768]{1,0:T(8,128)(2,1)S(1)}, u32[]{:S(2)}, u32[]{:S(2)}) collective-permute-start(bf16[256,768]{1,0:T(8,128)(2,1)S(1)} %get-tuple-element.62), channel_id=1, source_target_pairs={{0,48},{1,13},{4,52},{5,1},{8,56},{9,5},{12,60},{13,9},{16,0},{17,... | collective-permute-start | bytes 1179656 | tf_op jit(solution)/shard_map/ppermute | solution.py:27
  149.5 20.1 %collective-permute-start.36 = (bf16[256,768]{1,0:T(8,128)(2,1)S(1)}, bf16[256,768]{1,0:T(8,128)(2,1)S(1)}, u32[]{:S(2)}, u32[]{:S(2)}) collective-permute-start(bf16[256,768]{1,0:T(8,128)(2,1)S(1)} %get-tuple-element.58), channel_id=1, source_target_pairs={{0,16},{1,5},{4,20},{5,9},{8,24},{9,13},{12,28},{13,1},{16,32},{17... | collective-permute-start | bytes 1179656 | tf_op jit(solution)/shard_map/ppermute | solution.py:27
  149.5 31.4 %collective-permute-start.40 = (bf16[256,768]{1,0:T(8,128)(2,1)S(1)}, bf16[256,768]{1,0:T(8,128)(2,1)S(1)}, u32[]{:S(2)}, u32[]{:S(2)}) collective-permute-start(bf16[256,768]{1,0:T(8,128)(2,1)S(1)} %get-tuple-element.52), channel_id=1, source_target_pairs={{0,16},{1,5},{4,20},{5,9},{8,24},{9,13},{12,28},{13,1},{16,32},{17... | collective-permute-start | bytes 1179656 | tf_op jit(solution)/shard_map/ppermute | solution.py:27
  164.8 20.0 %collective-permute-start.32 = (bf16[192,1024]{1,0:T(8,128)(2,1)S(1)}, bf16[192,1024]{1,0:T(8,128)(2,1)S(1)}, u32[]{:S(2)}, u32[]{:S(2)}) collective-permute-start(bf16[192,1024]{1,0:T(8,128)(2,1)S(1)} %get-tuple-element.26), channel_id=1, source_target_pairs={{0,4},{1,17},{4,8},{5,21},{8,12},{9,25},{12,0},{13,29},{16,20},{17... | collective-permute-start | bytes 1179656 | tf_op jit(solution)/shard_map/ppermute | solution.py:23
  165.0 21.2 %collective-permute-start.31 = (bf16[192,1024]{1,0:T(8,128)(2,1)S(1)}, bf16[192,1024]{1,0:T(8,128)(2,1)S(1)}, u32[]{:S(2)}, u32[]{:S(2)}) collective-permute-start(bf16[192,1024]{1,0:T(8,128)(2,1)S(1)} %get-tuple-element.27), channel_id=1, source_target_pairs={{0,8},{1,33},{4,12},{5,37},{8,0},{9,41},{12,4},{13,45},{16,24},{17... | collective-permute-start | bytes 1179656 | tf_op jit(solution)/shard_map/ppermute | solution.py:23
  165.3 22.8 %collective-permute-start.30 = (bf16[192,1024]{1,0:T(8,128)(2,1)S(1)}, bf16[192,1024]{1,0:T(8,128)(2,1)S(1)}, u32[]{:S(2)}, u32[]{:S(2)}) collective-permute-start(bf16[192,1024]{1,0:T(8,128)(2,1)S(1)} %get-tuple-element.25), channel_id=1, source_target_pairs={{0,12},{1,49},{4,0},{5,53},{8,4},{9,57},{12,8},{13,61},{16,28},{17... | collective-permute-start | bytes 1179656 | tf_op jit(solution)/shard_map/ppermute | solution.py:23
  174.8 13.9 %collective-permute-start.37 = (bf16[384,768]{1,0:T(8,128)(2,1)S(1)}, bf16[384,768]{1,0:T(8,128)(2,1)S(1)}, u32[]{:S(2)}, u32[]{:S(2)}) collective-permute-start(bf16[384,768]{1,0:T(8,128)(2,1)S(1)} %pad_maximum_fusion.14), channel_id=1, source_target_pairs={{0,12},{1,49},{4,0},{5,53},{8,4},{9,57},{12,8},{13,61},{16,28},{17... | collective-permute-start | bytes 1769480 | tf_op jit(solution)/shard_map/ppermute | solution.py:23
  184.7 14.0 %collective-permute-start.39 = (bf16[384,768]{1,0:T(8,128)(2,1)S(1)}, bf16[384,768]{1,0:T(8,128)(2,1)S(1)}, u32[]{:S(2)}, u32[]{:S(2)}) collective-permute-start(bf16[384,768]{1,0:T(8,128)(2,1)S(1)} %pad_maximum_fusion.16), channel_id=1, source_target_pairs={{0,4},{1,17},{4,8},{5,21},{8,12},{9,25},{12,0},{13,29},{16,20},{17... | collective-permute-start | bytes 1769480 | tf_op jit(solution)/shard_map/ppermute | solution.py:23
  186.2 15.3 %collective-permute-start.41 = (bf16[384,768]{1,0:T(8,128)(2,1)S(1)}, bf16[384,768]{1,0:T(8,128)(2,1)S(1)}, u32[]{:S(2)}, u32[]{:S(2)}) collective-permute-start(bf16[384,768]{1,0:T(8,128)(2,1)S(1)} %pad_maximum_fusion.17), channel_id=1, source_target_pairs={{0,12},{1,49},{4,0},{5,53},{8,4},{9,57},{12,8},{13,61},{16,28},{17... | collective-permute-start | bytes 1769480 | tf_op jit(solution)/shard_map/ppermute | solution.py:23
  188.1 17.1 %collective-permute-start.42 = (bf16[384,768]{1,0:T(8,128)(2,1)S(1)}, bf16[384,768]{1,0:T(8,128)(2,1)S(1)}, u32[]{:S(2)}, u32[]{:S(2)}) collective-permute-start(bf16[384,768]{1,0:T(8,128)(2,1)S(1)} %pad_maximum_fusion.18), channel_id=1, source_target_pairs={{0,8},{1,33},{4,12},{5,37},{8,0},{9,41},{12,4},{13,45},{16,24},{17... | collective-permute-start | bytes 1769480 | tf_op jit(solution)/shard_map/ppermute | solution.py:23
  188.7 22.6 %collective-permute-start.43 = (bf16[384,768]{1,0:T(8,128)(2,1)S(1)}, bf16[384,768]{1,0:T(8,128)(2,1)S(1)}, u32[]{:S(2)}, u32[]{:S(2)}) collective-permute-start(bf16[384,768]{1,0:T(8,128)(2,1)S(1)} %pad_maximum_fusion.19), channel_id=1, source_target_pairs={{0,4},{1,17},{4,8},{5,21},{8,12},{9,25},{12,0},{13,29},{16,20},{17... | collective-permute-start | bytes 1769480 | tf_op jit(solution)/shard_map/ppermute | solution.py:23
  (48 other events, 513.7 us)
where the time goes:
time: 215 us; the launch traced here: 214 us
  waiting for transfers between devices  83.3 us (39%)
  starting transfers between devices  75.1 us (35%)
  other arithmetic  25 us (12%)
  local copies, waits for them, and re-layouts  15.2 us (7%)
  matrix products  14.2 us (7%)
    ppermute x16, waiting for transfers between devices, pass_on(): return lax.ppermute(value, ('z', 'x', 'c'), ring(step, False))  32.8 us
    ppermute x18, waiting for transfers between devices, deal(): return lax.ppermute(value, ('z', 'x', 'c'), ring(step, True))  29.7 us
    ppermute x18, starting transfers between devices, deal(): return lax.ppermute(value, ('z', 'x', 'c'), ring(step, True))  26.7 us
    ppermute x16, starting transfers between devices, pass_on(): return lax.ppermute(value, ('z', 'x', 'c'), ring(step, False))  25.9 us
    ppermute x10, starting transfers between devices, swap(): return lax.ppermute(value, axis, SWAP)  22.5 us
    ppermute x10, waiting for transfers between devices, swap(): return lax.ppermute(value, axis, SWAP)  20.9 us
    dot_general x8, matrix products, mul(): return lax.dot_general(a, b, dims, preferred_element_type=f32).astype(bf16)  11.4 us
    dynamic_update_slice x8, other arithmetic, local(): lax.dynamic_update_slice(grad_down, piece[rows:].astype(f32), (0, at))  8.23 us
  transfers between devices with their start and end apart: 44, of which 22 were waited for; matrix products, arithmetic and copies ran while one was open for 22% of the time, Pallas kernels for 0%

commit v1 on v0

v1 whole, which is shorter than its diff:
```python
import jax
import jax.numpy as jnp
from jax import lax
from jax.experimental import pallas as pl
from jax.sharding import Mesh
from jax.sharding import PartitionSpec as P

AXES = ("yh", "z", "x", "yl", "c")
CHUNKS = 2
SWAP = [(0, 1), (1, 0)]
F32 = jnp.float32
BF16 = jnp.bfloat16


def ring(step, along_x):
    pairs = []
    for z in range(4):
        for x in range(4):
            for c in range(2):
                to = (z, (x + step) % 4) if (c == 0) == along_x else ((z + step) % 4, x)
                pairs.append(((z * 4 + x) * 2 + c, (to[0] * 4 + to[1]) * 2 + c))
    return pairs


def deal(value, step):
    return lax.ppermute(value, ("z", "x", "c"), ring(step, True))


def pass_on(value, step):
    return lax.ppermute(value, ("z", "x", "c"), ring(step, False))


def swap(value, axis):
    return lax.ppermute(value, axis, SWAP)


def after(values, *others):
    return lax.optimization_barrier((tuple(values), others))[0]


def ordered(first, mine, other, axis):
    return jnp.where(
        first, jnp.concatenate([mine, other], axis), jnp.concatenate([other, mine], axis)
    )


def halves(value, index, axis):
    half = value.shape[axis] // 2
    return (
        lax.dynamic_slice_in_dim(value, index * half, half, axis),
        lax.dynamic_slice_in_dim(value, (1 - index) * half, half, axis),
    )


def rotated(value, by):
    width = value.shape[-1]
    return lax.dynamic_slice_in_dim(
        jnp.concatenate([value, value], -1), by * (width // 4), width, value.ndim - 1
    )


def mul(a, b, left, right):
    return lax.dot_general(a, b, (((left,), (right,)), ((), ())), preferred_element_type=F32)


def activate(preact, grad_act):
    activation, pullback = jax.vjp(lambda value: jax.nn.gelu(value, approximate=True), preact)
    grad_pre = pullback(grad_act)[0]
    return jnp.stack([grad_pre.astype(BF16), activation.astype(BF16)])


def weight_piece(up, down, at, width):
    return jnp.concatenate([lax.dynamic_slice_in_dim(w, at, width, 1) for w in (up, down)], 0)


def unwritten(shape):
    return pl.pallas_call(
        lambda out: None,
        out_shape=jax.ShapeDtypeStruct(shape, F32),
        out_specs=pl.BlockSpec(memory_space=pl.ANY),
    )()


def local(tokens, out_grad, up, down):
    tok, yl, core = lax.axis_index("yh"), lax.axis_index("yl"), lax.axis_index("c")
    x, z = lax.axis_index("x"), lax.axis_index("z")
    dealt = jnp.where(core == 0, x, z)
    summed = jnp.where(core == 0, z, x)
    rows = up.shape[0]
    whole = up.shape[1] // 4
    width = whole // CHUNKS
    order = (1, 3, 2)
    starts = {k: lax.rem(dealt + k, 4) * whole for k in range(4)}

    turned = jnp.stack([tokens.T, out_grad.T])
    held, other = halves(turned, tok, 1)
    got = [deal(weight_piece(up, down, starts[k], whole), k) for k in order]
    held = ordered(tok == 0, held, swap(other, "yh"), 2)
    held = ordered(yl == 0, held, swap(held, "yl"), 2)
    held = ordered(core == 0, held, swap(held, "c"), 2)
    held = rotated(held, summed)
    (held,) = after((held,), *got)
    parts = [held] + [deal(held, k) for k in order]
    got = [weight_piece(*after((up, down), held), starts[0], whole)] + got
    weights = [jnp.concatenate([w[i * rows : (i + 1) * rows] for w in got], 0) for i in range(2)]
    weights = [[w[:, j * width : (j + 1) * width] for w in weights] for j in range(CHUNKS)]
    columns = [jnp.concatenate([p[i] for p in parts], 0) for i in range(2)]

    shares = []
    for j in range(CHUNKS):
        pre, act = (
            mul(columns[i], weights[j][i], 0, 0).astype(BF16).reshape(4, -1, width) for i in range(2)
        )
        pre_in, act_in = pass_on(pre[2], 1), pass_on(act[2], -1)
        later = jnp.stack([(pre[1].astype(F32) + pre_in.astype(F32)).astype(BF16), act[1]])
        before = jnp.stack([pre[3], (act[3].astype(F32) + act_in.astype(F32)).astype(BF16)])
        total = jnp.stack([pre[0], act[0]]).astype(F32)
        total = total + pass_on(later, 1).astype(F32) + pass_on(before, -1).astype(F32)
        total = total + swap(total.astype(BF16), "yh").astype(F32)
        shares.append(activate(total[0], total[1]))

    grads = []
    part = 0.0
    for j in range(CHUNKS):
        mine = shares[j]
        from_before, from_after = pass_on(mine, 1), pass_on(mine, -1)
        far = (pass_on(from_before[0], 1), pass_on(from_after[1], -1))
        full = [
            jnp.concatenate([mine[i], from_after[i], far[i], from_before[i]], 0) for i in range(2)
        ]
        grads.append([mul(columns[i], full[i], 1, 0).astype(BF16) for i in range(2)])
        part += mul(weights[j][0], full[0], 1, 1)
    part = part.astype(BF16)

    total = part[:rows].astype(F32)
    for i, k in enumerate(order, 1):
        total = total + deal(part[i * rows : (i + 1) * rows], -k).astype(F32)
    total = rotated(total, lax.rem(4 - summed, 4))
    for axis, at in (("c", core), ("yl", yl)):
        mine, other = halves(total, at, 1)
        total = mine + swap(other.astype(BF16), axis).astype(F32)
    mine, other = halves(total.astype(BF16), tok, 1)
    grad_tokens = ordered(tok == 0, mine, swap(other, "yh"), 0).T

    outs = [unwritten(up.shape) for _ in range(2)]
    for j in range(CHUNKS):
        for i, k in enumerate((0,) + order):
            piece = jnp.concatenate([g[i * rows : (i + 1) * rows] for g in grads[j]], 0)
            if i:
                piece = deal(piece, -k)
            at = (0, starts[k] + j * width)
            outs = [
                lax.dynamic_update_slice(o, p.astype(F32), at)
                for o, p in zip(outs, (piece[:rows], piece[rows:]))
            ]
    return (grad_tokens, *outs)


def solution(mesh):
    cube = Mesh(mesh.devices.reshape(2, 4, 4, 2, 2), AXES)
    rows = P(("yh", "yl", "c"), ("z", "x"))
    weight = P(("z", "x", "yh"), ("yl", "c"))
    return jax.shard_map(
        local,
        mesh=cube,
        in_specs=(rows, rows, weight, weight),
        out_specs=(rows, weight, weight),
        check_vma=False,
    )
```

time: 215 us -> 205 us (0.953)
  starting transfers between devices: 75.1 us -> 57.3 us
  waiting for transfers between devices: 83.3 us -> 94.9 us
  local copies, waits for them, and re-layouts: 15.2 us -> 10.9 us
    ppermute x10 -> x8, starting transfers between devices: 22.5 us -> 7.14 us  [swap(): return lax.ppermute(value, axis, SWAP)]
    ppermute x10 -> x8, waiting for transfers between devices: 20.9 us -> 31.6 us  [swap(): return lax.ppermute(value, axis, SWAP)]
    ppermute x18 -> x15, waiting for transfers between devices: 29.7 us -> 36.5 us  [deal(): return lax.ppermute(value, ('z', 'x', 'c'), ring(step, True))]
    ppermute x16, waiting for transfers between devices: 32.8 us -> 26.7 us  [pass_on(): return lax.ppermute(value, ('z', 'x', 'c'), ring(step, False))]
    another operation x6 -> x0, local copies, waits for them, and re-layouts: 5.86 us -> none
    ppermute x18 -> x15, starting transfers between devices: 26.7 us -> 21.3 us  [deal(): return lax.ppermute(value, ('z', 'x', 'c'), ring(step, True))]
    convert_element_type x3 -> x8, other arithmetic: 0.6 us -> 4.92 us  [the longest x2 2.42 us: local(): total = total + swap(total.astype(BF16), 'yh').astype(F32)]
    another operation x11, other arithmetic: 4.97 us -> 0.88 us  [the longest x4 0.36 us: local(): jnp.stack([pre[3], (act[3].astype(F32) + act_in.astype(F32)).astype(BF16)])]
  transfers between devices with their start and end apart: 44 -> 39, of which waited for: 22 -> 24; matrix products, arithmetic and copies ran while one was open for 22% -> 19% of each run, Pallas kernels for 0% -> 0%
where the time goes in v1:
time: 205 us; the launch traced here: 203 us
  waiting for transfers between devices  94.9 us (46%)
  starting transfers between devices  57.3 us (28%)
  other arithmetic  24.1 us (12%)
  matrix products  14.3 us (7%)
  local copies, waits for them, and re-layouts  10.9 us (5%)
    ppermute x15, waiting for transfers between devices, deal(): return lax.ppermute(value, ('z', 'x', 'c'), ring(step, True))  36.5 us
    ppermute x8, waiting for transfers between devices, swap(): return lax.ppermute(value, axis, SWAP)  31.6 us
    ppermute x16, starting transfers between devices, pass_on(): return lax.ppermute(value, ('z', 'x', 'c'), ring(step, False))  28.8 us
    ppermute x16, waiting for transfers between devices, pass_on(): return lax.ppermute(value, ('z', 'x', 'c'), ring(step, False))  26.7 us
    ppermute x15, starting transfers between devices, deal(): return lax.ppermute(value, ('z', 'x', 'c'), ring(step, True))  21.3 us
    dot_general x10, matrix products, mul(): lax.dot_general(a, b, (((left,), (right,)), ((), ())), preferred_element_...  14.3 us
    dynamic_update_slice x10, other arithmetic, local(): lax.dynamic_update_slice(o, p.astype(F32), at)  9.94 us
    ppermute x8, starting transfers between devices, swap(): return lax.ppermute(value, axis, SWAP)  7.14 us
  transfers between devices with their start and end apart: 39, of which 24 were waited for; matrix products, arithmetic and copies ran while one was open for 19% of the time, Pallas kernels for 0%

profile of v1, /device:TPU:0, one launch (start us, length us, event | category | flops | bytes accessed | tf_op | source)
XLA Modules:
  0.0 202.9 jit_solution(14587010004899883732)
XLA Ops:
  2.7 3.4 %collective-permute-start = (bf16[2,192,128]{2,1,0:T(8,128)(2,1)S(1)}, bf16[2,192,128]{2,1,0:T(8,128)(2,1)S(1)}, u32[]{:S(2)}, u32[]{:S(2)}) collective-permute-start(bf16[2,192,128]{2,1,0:T(8,128)(2,1)S(1)} %get-tuple-element.91), channel_id=1, source_target_pairs={{0,64},{64,0},{1,65},{65,1},{2,66},{66,2},{3,67},{67,3},{4,68},{68... | collective-permute-start | bytes 294920 | tf_op jit(solution)/shard_map/ppermute | solution.py:34
  9.3 3.0 %collective-permute-start.5 = (bf16[384,1536]{1,0:T(8,128)(2,1)}, bf16[384,1536]{1,0:T(8,128)(2,1)S(1)}, u32[]{:S(2)}, u32[]{:S(2)}) collective-permute-start(bf16[384,1536]{1,0:T(8,128)(2,1)} %pad_maximum_fusion.8), channel_id=1, source_target_pairs={{0,8},{1,33},{4,12},{5,37},{8,0},{9,41},{12,4},{13,45},{16,24},{17... | collective-permute-start | bytes 3538952 | tf_op jit(solution)/shard_map/ppermute | solution.py:26
  17.4 5.7 %collective-permute-done.1 = bf16[2,192,256]{2,1,0:T(8,128)(2,1)S(1)} collective-permute-done((bf16[2,192,256]{2,1,0:T(8,128)(2,1)S(1)}, bf16[2,192,256]{2,1,0:T(8,128)(2,1)S(1)}, u32[]{:S(2)}, u32[]{:S(2)}) %collective-permute-start.1) | collective-permute-done | bytes 196640 | tf_op jit(solution)/shard_map/ppermute | solution.py:34
  27.4 12.7 %collective-permute-done.4 = bf16[384,1536]{1,0:T(8,128)(2,1)S(1)} collective-permute-done((bf16[384,1536]{1,0:T(8,128)(2,1)}, bf16[384,1536]{1,0:T(8,128)(2,1)S(1)}, u32[]{:S(2)}, u32[]{:S(2)}) %collective-permute-start.4) | collective-permute-done | bytes 1179680 | tf_op jit(solution)/shard_map/ppermute | solution.py:26
  40.0 3.0 %collective-permute-start.8 = (bf16[2,192,1024]{2,1,0:T(8,128)(2,1)S(1)}, bf16[2,192,1024]{2,1,0:T(8,128)(2,1)S(1)}, u32[]{:S(2)}, u32[]{:S(2)}) collective-permute-start(bf16[2,192,1024]{2,1,0:T(8,128)(2,1)S(1)} %fusion.59), channel_id=1, source_target_pairs={{0,8},{1,33},{4,12},{5,37},{8,0},{9,41},{12,4},{13,45},{16,24},{17... | collective-permute-start | bytes 2359304 | tf_op jit(solution)/shard_map/ppermute | solution.py:26
  49.2 4.5 %collective-permute-done.8 = bf16[2,192,1024]{2,1,0:T(8,128)(2,1)S(1)} collective-permute-done((bf16[2,192,1024]{2,1,0:T(8,128)(2,1)S(1)}, bf16[2,192,1024]{2,1,0:T(8,128)(2,1)S(1)}, u32[]{:S(2)}, u32[]{:S(2)}) %collective-permute-start.8) | collective-permute-done | bytes 786464 | tf_op jit(solution)/shard_map/ppermute | solution.py:26
  53.7 8.2 %collective-permute-done.7 = bf16[2,192,1024]{2,1,0:T(8,128)(2,1)S(1)} collective-permute-done((bf16[2,192,1024]{2,1,0:T(8,128)(2,1)S(1)}, bf16[2,192,1024]{2,1,0:T(8,128)(2,1)S(1)}, u32[]{:S(2)}, u32[]{:S(2)}) %collective-permute-start.7) | collective-permute-done | bytes 786464 | tf_op jit(solution)/shard_map/ppermute | solution.py:26
  72.9 3.3 %collective-permute-start.19 = (bf16[256,768]{1,0:T(8,128)(2,1)S(1)}, bf16[256,768]{1,0:T(8,128)(2,1)S(1)}, u32[]{:S(2)}, u32[]{:S(2)}) collective-permute-start(bf16[256,768]{1,0:T(8,128)(2,1)S(1)} %get-tuple-element.42), channel_id=1, source_target_pairs={{0,48},{1,13},{4,52},{5,1},{8,56},{9,5},{12,60},{13,9},{16,0},{17,... | collective-permute-start | bytes 1179656 | tf_op jit(solution)/shard_map/ppermute | solution.py:30
  78.5 3.4 %collective-permute-start.12 = (bf16[2,256,768]{2,1,0:T(8,128)(2,1)S(1)}, bf16[2,256,768]{2,1,0:T(8,128)(2,1)S(1)}, u32[]{:S(2)}, u32[]{:S(2)}) collective-permute-start(bf16[2,256,768]{2,1,0:T(8,128)(2,1)S(1)} %pad_maximum_fusion.11), channel_id=1, source_target_pairs={{0,48},{1,13},{4,52},{5,1},{8,56},{9,5},{12,60},{13,9},{16,0},{17,... | collective-permute-start | bytes 2359304 | tf_op jit(solution)/shard_map/ppermute | solution.py:30
  82.8 3.4 %collective-permute-start.20 = (bf16[2,256,768]{2,1,0:T(8,128)(2,1)S(1)}, bf16[2,256,768]{2,1,0:T(8,128)(2,1)S(1)}, u32[]{:S(2)}, u32[]{:S(2)}) collective-permute-start(bf16[2,256,768]{2,1,0:T(8,128)(2,1)S(1)} %pad_maximum_fusion.15), channel_id=1, source_target_pairs={{0,48},{1,13},{4,52},{5,1},{8,56},{9,5},{12,60},{13,9},{16,0},{17,... | collective-permute-start | bytes 2359304 | tf_op jit(solution)/shard_map/ppermute | solution.py:30
  86.4 5.0 %collective-permute-done.12 = bf16[2,256,768]{2,1,0:T(8,128)(2,1)S(1)} collective-permute-done((bf16[2,256,768]{2,1,0:T(8,128)(2,1)S(1)}, bf16[2,256,768]{2,1,0:T(8,128)(2,1)S(1)}, u32[]{:S(2)}, u32[]{:S(2)}) %collective-permute-start.12) | collective-permute-done | bytes 786464 | tf_op jit(solution)/shard_map/ppermute | solution.py:30
  91.4 4.3 %collective-permute-done.10 = bf16[2,256,768]{2,1,0:T(8,128)(2,1)S(1)} collective-permute-done((bf16[2,256,768]{2,1,0:T(8,128)(2,1)S(1)}, bf16[2,256,768]{2,1,0:T(8,128)(2,1)S(1)}, u32[]{:S(2)}, u32[]{:S(2)}) %collective-permute-start.10) | collective-permute-done | bytes 786464 | tf_op jit(solution)/shard_map/ppermute | solution.py:30
  99.9 4.3 %collective-permute-done.18 = bf16[2,256,768]{2,1,0:T(8,128)(2,1)S(1)} collective-permute-done((bf16[2,256,768]{2,1,0:T(8,128)(2,1)S(1)}, bf16[2,256,768]{2,1,0:T(8,128)(2,1)S(1)}, u32[]{:S(2)}, u32[]{:S(2)}) %collective-permute-start.18) | collective-permute-done | bytes 786464 | tf_op jit(solution)/shard_map/ppermute | solution.py:30
  106.5 12.8 %collective-permute-done.13 = bf16[2,256,768]{2,1,0:T(8,128)(2,1)} collective-permute-done((bf16[2,256,768]{2,1,0:T(8,128)(2,1)}, bf16[2,256,768]{2,1,0:T(8,128)(2,1)}, u32[]{:S(2)}, u32[]{:S(2)}) %collective-permute-start.13) | collective-permute-done | bytes 786464 | tf_op jit(solution)/shard_map/ppermute | solution.py:34
  121.8 3.2 %collective-permute-start.14 = (bf16[2,256,768]{2,1,0:T(8,128)(2,1)S(1)}, bf16[2,256,768]{2,1,0:T(8,128)(2,1)S(1)}, u32[]{:S(2)}, u32[]{:S(2)}) collective-permute-start(bf16[2,256,768]{2,1,0:T(8,128)(2,1)S(1)} %pad_maximum_fusion.12), channel_id=1, source_target_pairs={{0,48},{1,13},{4,52},{5,1},{8,56},{9,5},{12,60},{13,9},{16,0},{17,... | collective-permute-start | bytes 2359304 | tf_op jit(solution)/shard_map/ppermute | solution.py:30
  125.0 6.8 %collective-permute-done.21 = bf16[2,256,768]{2,1,0:T(8,128)(2,1)} collective-permute-done((bf16[2,256,768]{2,1,0:T(8,128)(2,1)}, bf16[2,256,768]{2,1,0:T(8,128)(2,1)}, u32[]{:S(2)}, u32[]{:S(2)}) %collective-permute-start.21) | collective-permute-done | bytes 786464 | tf_op jit(solution)/shard_map/ppermute | solution.py:34
  135.0 2.9 %collective-permute-start.22 = (bf16[2,256,768]{2,1,0:T(8,128)(2,1)S(1)}, bf16[2,256,768]{2,1,0:T(8,128)(2,1)S(1)}, u32[]{:S(2)}, u32[]{:S(2)}) collective-permute-start(bf16[2,256,768]{2,1,0:T(8,128)(2,1)S(1)} %pad_maximum_fusion.16), channel_id=1, source_target_pairs={{0,48},{1,13},{4,52},{5,1},{8,56},{9,5},{12,60},{13,9},{16,0},{17,... | collective-permute-start | bytes 2359304 | tf_op jit(solution)/shard_map/ppermute | solution.py:30
  138.7 3.3 %collective-permute-start.31 = (bf16[256,768]{1,0:T(8,128)(2,1)S(1)}, bf16[256,768]{1,0:T(8,128)(2,1)S(1)}, u32[]{:S(2)}, u32[]{:S(2)}) collective-permute-start(bf16[256,768]{1,0:T(8,128)(2,1)S(1)} %get-tuple-element.66), channel_id=1, source_target_pairs={{0,48},{1,13},{4,52},{5,1},{8,56},{9,5},{12,60},{13,9},{16,0},{17,... | collective-permute-start | bytes 1179656 | tf_op jit(solution)/shard_map/ppermute | solution.py:30
  142.0 5.2 %collective-permute-done.23 = bf16[2,256,768]{2,1,0:T(8,128)(2,1)S(1)} collective-permute-done((bf16[2,256,768]{2,1,0:T(8,128)(2,1)S(1)}, bf16[2,256,768]{2,1,0:T(8,128)(2,1)S(1)}, u32[]{:S(2)}, u32[]{:S(2)}) %collective-permute-start.23) | collective-permute-done | bytes 786464 | tf_op jit(solution)/shard_map/ppermute | solution.py:30
  147.5 4.0 %collective-permute-start.35 = (bf16[256,768]{1,0:T(8,128)(2,1)S(1)}, bf16[256,768]{1,0:T(8,128)(2,1)S(1)}, u32[]{:S(2)}, u32[]{:S(2)}) collective-permute-start(bf16[256,768]{1,0:T(8,128)(2,1)S(1)} %get-tuple-element.62), channel_id=1, source_target_pairs={{0,48},{1,13},{4,52},{5,1},{8,56},{9,5},{12,60},{13,9},{16,0},{17,... | collective-permute-start | bytes 1179656 | tf_op jit(solution)/shard_map/ppermute | solution.py:30
  156.9 2.6 %collective-permute-done.35 = bf16[256,768]{1,0:T(8,128)(2,1)S(1)} collective-permute-done((bf16[256,768]{1,0:T(8,128)(2,1)S(1)}, bf16[256,768]{1,0:T(8,128)(2,1)S(1)}, u32[]{:S(2)}, u32[]{:S(2)}) %collective-permute-start.35) | collective-permute-done | bytes 393248 | tf_op jit(solution)/shard_map/ppermute | solution.py:30
  169.6 3.8 %collective-permute-done.25 = bf16[192,1024]{1,0:T(8,128)(2,1)S(1)} collective-permute-done((bf16[192,1024]{1,0:T(8,128)(2,1)S(1)}, bf16[192,1024]{1,0:T(8,128)(2,1)S(1)}, u32[]{:S(2)}, u32[]{:S(2)}) %collective-permute-start.25) | collective-permute-done | bytes 393248 | tf_op jit(solution)/shard_map/ppermute | solution.py:26
  175.1 5.2 %collective-permute-start.36 = (bf16[384,768]{1,0:T(8,128)(2,1)S(1)}, bf16[384,768]{1,0:T(8,128)(2,1)S(1)}, u32[]{:S(2)}, u32[]{:S(2)}) collective-permute-start(bf16[384,768]{1,0:T(8,128)(2,1)S(1)} %pad_maximum_fusion.20), channel_id=1, source_target_pairs={{0,12},{1,49},{4,0},{5,53},{8,4},{9,57},{12,8},{13,61},{16,28},{17... | collective-permute-start | bytes 1769480 | tf_op jit(solution)/shard_map/ppermute | solution.py:26
  199.3 2.8 %collective-permute-done.30 = bf16[192,128]{1,0:T(8,128)(2,1)S(1)} collective-permute-done((bf16[192,128]{1,0:T(8,128)(2,1)S(1)}, bf16[192,128]{1,0:T(8,128)(2,1)S(1)}, u32[]{:S(2)}, u32[]{:S(2)}) %collective-permute-start.30) | collective-permute-done | bytes 49184 | tf_op jit(solution)/shard_map/ppermute | solution.py:34
  (181 shorter events, 84.7 us)
Async XLA Ops:
  2.7 13.9 %collective-permute-start = (bf16[2,192,128]{2,1,0:T(8,128)(2,1)S(1)}, bf16[2,192,128]{2,1,0:T(8,128)(2,1)S(1)}, u32[]{:S(2)}, u32[]{:S(2)}) collective-permute-start(bf16[2,192,128]{2,1,0:T(8,128)(2,1)S(1)} %get-tuple-element.91), channel_id=1, source_target_pairs={{0,64},{64,0},{1,65},{65,1},{2,66},{66,2},{3,67},{67,3},{4,68},{68... | collective-permute-start | bytes 294920 | tf_op jit(solution)/shard_map/ppermute | solution.py:34
  9.3 18.0 %collective-permute-start.5 = (bf16[384,1536]{1,0:T(8,128)(2,1)}, bf16[384,1536]{1,0:T(8,128)(2,1)S(1)}, u32[]{:S(2)}, u32[]{:S(2)}) collective-permute-start(bf16[384,1536]{1,0:T(8,128)(2,1)} %pad_maximum_fusion.8), channel_id=1, source_target_pairs={{0,8},{1,33},{4,12},{5,37},{8,0},{9,41},{12,4},{13,45},{16,24},{17... | collective-permute-start | bytes 3538952 | tf_op jit(solution)/shard_map/ppermute | solution.py:26
  13.5 26.6 %collective-permute-start.4 = (bf16[384,1536]{1,0:T(8,128)(2,1)}, bf16[384,1536]{1,0:T(8,128)(2,1)S(1)}, u32[]{:S(2)}, u32[]{:S(2)}) collective-permute-start(bf16[384,1536]{1,0:T(8,128)(2,1)} %pad_maximum_fusion.7), channel_id=1, source_target_pairs={{0,12},{1,49},{4,0},{5,53},{8,4},{9,57},{12,8},{13,61},{16,28},{17... | collective-permute-start | bytes 3538952 | tf_op jit(solution)/shard_map/ppermute | solution.py:26
  15.7 24.3 %collective-permute-start.3 = (bf16[384,1536]{1,0:T(8,128)(2,1)}, bf16[384,1536]{1,0:T(8,128)(2,1)}, u32[]{:S(2)}, u32[]{:S(2)}) collective-permute-start(bf16[384,1536]{1,0:T(8,128)(2,1)} %pad_maximum_fusion.6), channel_id=1, source_target_pairs={{0,4},{1,17},{4,8},{5,21},{8,12},{9,25},{12,0},{13,29},{16,20},{17... | collective-permute-start | bytes 3538952 | tf_op jit(solution)/shard_map/ppermute | solution.py:26
  40.0 13.6 %collective-permute-start.8 = (bf16[2,192,1024]{2,1,0:T(8,128)(2,1)S(1)}, bf16[2,192,1024]{2,1,0:T(8,128)(2,1)S(1)}, u32[]{:S(2)}, u32[]{:S(2)}) collective-permute-start(bf16[2,192,1024]{2,1,0:T(8,128)(2,1)S(1)} %fusion.59), channel_id=1, source_target_pairs={{0,8},{1,33},{4,12},{5,37},{8,0},{9,41},{12,4},{13,45},{16,24},{17... | collective-permute-start | bytes 2359304 | tf_op jit(solution)/shard_map/ppermute | solution.py:26
  43.0 18.9 %collective-permute-start.7 = (bf16[2,192,1024]{2,1,0:T(8,128)(2,1)S(1)}, bf16[2,192,1024]{2,1,0:T(8,128)(2,1)S(1)}, u32[]{:S(2)}, u32[]{:S(2)}) collective-permute-start(bf16[2,192,1024]{2,1,0:T(8,128)(2,1)S(1)} %fusion.59), channel_id=1, source_target_pairs={{0,12},{1,49},{4,0},{5,53},{8,4},{9,57},{12,8},{13,61},{16,28},{17... | collective-permute-start | bytes 2359304 | tf_op jit(solution)/shard_map/ppermute | solution.py:26
  44.2 17.8 %collective-permute-start.6 = (bf16[2,192,1024]{2,1,0:T(8,128)(2,1)S(1)}, bf16[2,192,1024]{2,1,0:T(8,128)(2,1)S(1)}, u32[]{:S(2)}, u32[]{:S(2)}) collective-permute-start(bf16[2,192,1024]{2,1,0:T(8,128)(2,1)S(1)} %fusion.59), channel_id=1, source_target_pairs={{0,4},{1,17},{4,8},{5,21},{8,12},{9,25},{12,0},{13,29},{16,20},{17... | collective-permute-start | bytes 2359304 | tf_op jit(solution)/shard_map/ppermute | solution.py:26
  68.2 17.9 %collective-permute-start.17 = (bf16[256,768]{1,0:T(8,128)(2,1)S(1)}, bf16[256,768]{1,0:T(8,128)(2,1)S(1)}, u32[]{:S(2)}, u32[]{:S(2)}) collective-permute-start(bf16[256,768]{1,0:T(8,128)(2,1)S(1)} %get-tuple-element.40), channel_id=1, source_target_pairs={{0,16},{1,5},{4,20},{5,9},{8,24},{9,13},{12,28},{13,1},{16,32},{17... | collective-permute-start | bytes 1179656 | tf_op jit(solution)/shard_map/ppermute | solution.py:30
  82.5 13.3 %collective-permute-start.10 = (bf16[2,256,768]{2,1,0:T(8,128)(2,1)S(1)}, bf16[2,256,768]{2,1,0:T(8,128)(2,1)S(1)}, u32[]{:S(2)}, u32[]{:S(2)}) collective-permute-start(bf16[2,256,768]{2,1,0:T(8,128)(2,1)S(1)} %pad_maximum_fusion.10), channel_id=1, source_target_pairs={{0,16},{1,5},{4,20},{5,9},{8,24},{9,13},{12,28},{13,1},{16,32},{17... | collective-permute-start | bytes 2359304 | tf_op jit(solution)/shard_map/ppermute | solution.py:30
  82.8 17.1 %collective-permute-start.20 = (bf16[2,256,768]{2,1,0:T(8,128)(2,1)S(1)}, bf16[2,256,768]{2,1,0:T(8,128)(2,1)S(1)}, u32[]{:S(2)}, u32[]{:S(2)}) collective-permute-start(bf16[2,256,768]{2,1,0:T(8,128)(2,1)S(1)} %pad_maximum_fusion.15), channel_id=1, source_target_pairs={{0,48},{1,13},{4,52},{5,1},{8,56},{9,5},{12,60},{13,9},{16,0},{17,... | collective-permute-start | bytes 2359304 | tf_op jit(solution)/shard_map/ppermute | solution.py:30
  86.3 17.9 %collective-permute-start.18 = (bf16[2,256,768]{2,1,0:T(8,128)(2,1)S(1)}, bf16[2,256,768]{2,1,0:T(8,128)(2,1)S(1)}, u32[]{:S(2)}, u32[]{:S(2)}) collective-permute-start(bf16[2,256,768]{2,1,0:T(8,128)(2,1)S(1)} %pad_maximum_fusion.14), channel_id=1, source_target_pairs={{0,16},{1,5},{4,20},{5,9},{8,24},{9,13},{12,28},{13,1},{16,32},{17... | collective-permute-start | bytes 2359304 | tf_op jit(solution)/shard_map/ppermute | solution.py:30
  97.0 22.3 %collective-permute-start.13 = (bf16[2,256,768]{2,1,0:T(8,128)(2,1)}, bf16[2,256,768]{2,1,0:T(8,128)(2,1)}, u32[]{:S(2)}, u32[]{:S(2)}) collective-permute-start(bf16[2,256,768]{2,1,0:T(8,128)(2,1)} %fusion.29), channel_id=1, source_target_pairs={{0,64},{64,0},{1,65},{65,1},{2,66},{66,2},{3,67},{67,3},{4,68},{68... | collective-permute-start | bytes 2359304 | tf_op jit(solution)/shard_map/ppermute | solution.py:34
  106.2 25.6 %collective-permute-start.21 = (bf16[2,256,768]{2,1,0:T(8,128)(2,1)}, bf16[2,256,768]{2,1,0:T(8,128)(2,1)}, u32[]{:S(2)}, u32[]{:S(2)}) collective-permute-start(bf16[2,256,768]{2,1,0:T(8,128)(2,1)} %fusion.30), channel_id=1, source_target_pairs={{0,64},{64,0},{1,65},{65,1},{2,66},{66,2},{3,67},{67,3},{4,68},{68... | collective-permute-start | bytes 2359304 | tf_op jit(solution)/shard_map/ppermute | solution.py:34
  121.7 16.8 %collective-permute-start.15 = (bf16[2,256,768]{2,1,0:T(8,128)(2,1)S(1)}, bf16[2,256,768]{2,1,0:T(8,128)(2,1)S(1)}, u32[]{:S(2)}, u32[]{:S(2)}) collective-permute-start(bf16[2,256,768]{2,1,0:T(8,128)(2,1)S(1)} %pad_maximum_fusion.12), channel_id=1, source_target_pairs={{0,16},{1,5},{4,20},{5,9},{8,24},{9,13},{12,28},{13,1},{16,32},{17... | collective-permute-start | bytes 2359304 | tf_op jit(solution)/shard_map/ppermute | solution.py:30
  121.8 16.9 %collective-permute-start.14 = (bf16[2,256,768]{2,1,0:T(8,128)(2,1)S(1)}, bf16[2,256,768]{2,1,0:T(8,128)(2,1)S(1)}, u32[]{:S(2)}, u32[]{:S(2)}) collective-permute-start(bf16[2,256,768]{2,1,0:T(8,128)(2,1)S(1)} %pad_maximum_fusion.12), channel_id=1, source_target_pairs={{0,48},{1,13},{4,52},{5,1},{8,56},{9,5},{12,60},{13,9},{16,0},{17,... | collective-permute-start | bytes 2359304 | tf_op jit(solution)/shard_map/ppermute | solution.py:30
  134.0 13.3 %collective-permute-start.23 = (bf16[2,256,768]{2,1,0:T(8,128)(2,1)S(1)}, bf16[2,256,768]{2,1,0:T(8,128)(2,1)S(1)}, u32[]{:S(2)}, u32[]{:S(2)}) collective-permute-start(bf16[2,256,768]{2,1,0:T(8,128)(2,1)S(1)} %pad_maximum_fusion.16), channel_id=1, source_target_pairs={{0,16},{1,5},{4,20},{5,9},{8,24},{9,13},{12,28},{13,1},{16,32},{17... | collective-permute-start | bytes 2359304 | tf_op jit(solution)/shard_map/ppermute | solution.py:30
  138.6 14.6 %collective-permute-start.16 = (bf16[256,768]{1,0:T(8,128)(2,1)S(1)}, bf16[256,768]{1,0:T(8,128)(2,1)S(1)}, u32[]{:S(2)}, u32[]{:S(2)}) collective-permute-start(bf16[256,768]{1,0:T(8,128)(2,1)S(1)} %get-tuple-element.69), channel_id=1, source_target_pairs={{0,16},{1,5},{4,20},{5,9},{8,24},{9,13},{12,28},{13,1},{16,32},{17... | collective-permute-start | bytes 1179656 | tf_op jit(solution)/shard_map/ppermute | solution.py:30
  147.3 13.7 %collective-permute-start.24 = (bf16[256,768]{1,0:T(8,128)(2,1)S(1)}, bf16[256,768]{1,0:T(8,128)(2,1)S(1)}, u32[]{:S(2)}, u32[]{:S(2)}) collective-permute-start(bf16[256,768]{1,0:T(8,128)(2,1)S(1)} %get-tuple-element.65), channel_id=1, source_target_pairs={{0,16},{1,5},{4,20},{5,9},{8,24},{9,13},{12,28},{13,1},{16,32},{17... | collective-permute-start | bytes 1179656 | tf_op jit(solution)/shard_map/ppermute | solution.py:30
  154.7 26.1 %collective-permute-start.32 = (bf16[384,768]{1,0:T(8,128)(2,1)S(1)}, bf16[384,768]{1,0:T(8,128)(2,1)S(1)}, u32[]{:S(2)}, u32[]{:S(2)}) collective-permute-start(bf16[384,768]{1,0:T(8,128)(2,1)S(1)} %pad_maximum_fusion.17), channel_id=1, source_target_pairs={{0,12},{1,49},{4,0},{5,53},{8,4},{9,57},{12,8},{13,61},{16,28},{17... | collective-permute-start | bytes 1769480 | tf_op jit(solution)/shard_map/ppermute | solution.py:26
  155.3 28.1 %collective-permute-start.33 = (bf16[384,768]{1,0:T(8,128)(2,1)S(1)}, bf16[384,768]{1,0:T(8,128)(2,1)S(1)}, u32[]{:S(2)}, u32[]{:S(2)}) collective-permute-start(bf16[384,768]{1,0:T(8,128)(2,1)S(1)} %pad_maximum_fusion.18), channel_id=1, source_target_pairs={{0,4},{1,17},{4,8},{5,21},{8,12},{9,25},{12,0},{13,29},{16,20},{17... | collective-permute-start | bytes 1769480 | tf_op jit(solution)/shard_map/ppermute | solution.py:26
  167.1 13.2 %collective-permute-start.26 = (bf16[192,1024]{1,0:T(8,128)(2,1)S(1)}, bf16[192,1024]{1,0:T(8,128)(2,1)S(1)}, u32[]{:S(2)}, u32[]{:S(2)}) collective-permute-start(bf16[192,1024]{1,0:T(8,128)(2,1)S(1)} %get-tuple-element.27), channel_id=1, source_target_pairs={{0,4},{1,17},{4,8},{5,21},{8,12},{9,25},{12,0},{13,29},{16,20},{17... | collective-permute-start | bytes 1179656 | tf_op jit(solution)/shard_map/ppermute | solution.py:26
  175.1 15.2 %collective-permute-start.36 = (bf16[384,768]{1,0:T(8,128)(2,1)S(1)}, bf16[384,768]{1,0:T(8,128)(2,1)S(1)}, u32[]{:S(2)}, u32[]{:S(2)}) collective-permute-start(bf16[384,768]{1,0:T(8,128)(2,1)S(1)} %pad_maximum_fusion.20), channel_id=1, source_target_pairs={{0,12},{1,49},{4,0},{5,53},{8,4},{9,57},{12,8},{13,61},{16,28},{17... | collective-permute-start | bytes 1769480 | tf_op jit(solution)/shard_map/ppermute | solution.py:26
  180.3 13.1 %collective-permute-start.37 = (bf16[384,768]{1,0:T(8,128)(2,1)S(1)}, bf16[384,768]{1,0:T(8,128)(2,1)S(1)}, u32[]{:S(2)}, u32[]{:S(2)}) collective-permute-start(bf16[384,768]{1,0:T(8,128)(2,1)S(1)} %pad_maximum_fusion.21), channel_id=1, source_target_pairs={{0,4},{1,17},{4,8},{5,21},{8,12},{9,25},{12,0},{13,29},{16,20},{17... | collective-permute-start | bytes 1769480 | tf_op jit(solution)/shard_map/ppermute | solution.py:26
  180.8 17.5 %collective-permute-start.38 = (bf16[384,768]{1,0:T(8,128)(2,1)S(1)}, bf16[384,768]{1,0:T(8,128)(2,1)S(1)}, u32[]{:S(2)}, u32[]{:S(2)}) collective-permute-start(bf16[384,768]{1,0:T(8,128)(2,1)S(1)} %pad_maximum_fusion.22), channel_id=1, source_target_pairs={{0,8},{1,33},{4,12},{5,37},{8,0},{9,41},{12,4},{13,45},{16,24},{17... | collective-permute-start | bytes 1769480 | tf_op jit(solution)/shard_map/ppermute | solution.py:26
  (34 other events, 281.3 us)

commit v2 on v1

--- a/solution.py
+++ b/solution.py
@@ -143,16 +143,16 @@
     grad_tokens = ordered(tok == 0, mine, swap(other, "yh"), 0).T
 
     outs = [unwritten(up.shape) for _ in range(2)]
-    for j in range(CHUNKS):
-        for i, k in enumerate((0,) + order):
-            piece = jnp.concatenate([g[i * rows : (i + 1) * rows] for g in grads[j]], 0)
-            if i:
-                piece = deal(piece, -k)
-            at = (0, starts[k] + j * width)
-            outs = [
-                lax.dynamic_update_slice(o, p.astype(F32), at)
-                for o, p in zip(outs, (piece[:rows], piece[rows:]))
-            ]
+    for i, k in enumerate((0,) + order):
+        rows_of = [[g[i * rows : (i + 1) * rows] for g in pair] for pair in grads]
+        piece = jnp.concatenate([jnp.concatenate(pair, 0) for pair in rows_of], 1)
+        if i:
+            piece = deal(piece, -k)
+        at = (0, starts[k])
+        outs = [
+            lax.dynamic_update_slice(o, p.astype(F32), at)
+            for o, p in zip(outs, (piece[:rows], piece[rows:]))
+        ]
     return (grad_tokens, *outs)
 
 

time: 205 us -> 207 us (level)
  starting transfers between devices: 57.3 us -> 50.7 us
  waiting for transfers between devices: 94.9 us -> 101 us
  local copies, waits for them, and re-layouts: 10.9 us -> 13.6 us
    ppermute x15 -> x12, starting transfers between devices: 21.3 us -> 16 us  [deal(): return lax.ppermute(value, ('z', 'x', 'c'), ring(step, True))]
    ppermute x8, waiting for transfers between devices: 31.6 us -> 36.5 us  [swap(): return lax.ppermute(value, axis, SWAP)]
    ppermute x15 -> x12, waiting for transfers between devices: 36.5 us -> 39.5 us  [deal(): return lax.ppermute(value, ('z', 'x', 'c'), ring(step, True))]
    unnamed x41, local copies, waits for them, and re-layouts: 3.91 us -> 6.51 us
    dynamic_update_slice x10 -> x4, other arithmetic: 9.94 us -> 10.5 us  [local(): lax.dynamic_update_slice(o, p.astype(F32), at)]
  transfers between devices with their start and end apart: 39 -> 36, of which waited for: 24 -> 24; matrix products, arithmetic and copies ran while one was open for 19% -> 17% of each run, Pallas kernels for 0% -> 0%
where the time goes in v2:
time: 207 us; the launch traced here: 206 us
  waiting for transfers between devices  101 us (49%)
  starting transfers between devices  50.7 us (24%)
  other arithmetic  25.4 us (12%)
  matrix products  14.2 us (7%)
  local copies, waits for them, and re-layouts  13.6 us (7%)
    ppermute x12, waiting for transfers between devices, deal(): return lax.ppermute(value, ('z', 'x', 'c'), ring(step, True))  39.5 us
    ppermute x8, waiting for transfers between devices, swap(): return lax.ppermute(value, axis, SWAP)  36.5 us
    ppermute x16, starting transfers between devices, pass_on(): return lax.ppermute(value, ('z', 'x', 'c'), ring(step, False))  28.8 us
    ppermute x16, waiting for transfers between devices, pass_on(): return lax.ppermute(value, ('z', 'x', 'c'), ring(step, False))  24.7 us
    ppermute x12, starting transfers between devices, deal(): return lax.ppermute(value, ('z', 'x', 'c'), ring(step, True))  16 us
    dot_general x10, matrix products, mul(): lax.dot_general(a, b, (((left,), (right,)), ((), ())), preferred_element_...  14.2 us
    dynamic_update_slice x4, other arithmetic, local(): lax.dynamic_update_slice(o, p.astype(F32), at)  10.5 us
    unnamed x41, local copies, waits for them, and re-layouts  6.51 us
  transfers between devices with their start and end apart: 36, of which 24 were waited for; matrix products, arithmetic and copies ran while one was open for 17% of the time, Pallas kernels for 0%

profile of v2, /device:TPU:0, one launch (start us, length us, event | category | flops | bytes accessed | tf_op | source)
XLA Modules:
  0.0 206.0 jit_solution(15907725257048454166)
XLA Ops:
  2.7 3.4 %collective-permute-start = (bf16[2,192,128]{2,1,0:T(8,128)(2,1)S(1)}, bf16[2,192,128]{2,1,0:T(8,128)(2,1)S(1)}, u32[]{:S(2)}, u32[]{:S(2)}) collective-permute-start(bf16[2,192,128]{2,1,0:T(8,128)(2,1)S(1)} %get-tuple-element.91), channel_id=1, source_target_pairs={{0,64},{64,0},{1,65},{65,1},{2,66},{66,2},{3,67},{67,3},{4,68},{68... | collective-permute-start | bytes 294920 | tf_op jit(solution)/shard_map/ppermute | solution.py:34
  9.3 3.0 %collective-permute-start.5 = (bf16[384,1536]{1,0:T(8,128)(2,1)}, bf16[384,1536]{1,0:T(8,128)(2,1)S(1)}, u32[]{:S(2)}, u32[]{:S(2)}) collective-permute-start(bf16[384,1536]{1,0:T(8,128)(2,1)} %pad_maximum_fusion.8), channel_id=1, source_target_pairs={{0,8},{1,33},{4,12},{5,37},{8,0},{9,41},{12,4},{13,45},{16,24},{17... | collective-permute-start | bytes 3538952 | tf_op jit(solution)/shard_map/ppermute | solution.py:26
  17.4 5.7 %collective-permute-done.1 = bf16[2,192,256]{2,1,0:T(8,128)(2,1)S(1)} collective-permute-done((bf16[2,192,256]{2,1,0:T(8,128)(2,1)S(1)}, bf16[2,192,256]{2,1,0:T(8,128)(2,1)S(1)}, u32[]{:S(2)}, u32[]{:S(2)}) %collective-permute-start.1) | collective-permute-done | bytes 196640 | tf_op jit(solution)/shard_map/ppermute | solution.py:34
  27.4 12.7 %collective-permute-done.4 = bf16[384,1536]{1,0:T(8,128)(2,1)S(1)} collective-permute-done((bf16[384,1536]{1,0:T(8,128)(2,1)}, bf16[384,1536]{1,0:T(8,128)(2,1)S(1)}, u32[]{:S(2)}, u32[]{:S(2)}) %collective-permute-start.4) | collective-permute-done | bytes 1179680 | tf_op jit(solution)/shard_map/ppermute | solution.py:26
  40.0 3.0 %collective-permute-start.8 = (bf16[2,192,1024]{2,1,0:T(8,128)(2,1)S(1)}, bf16[2,192,1024]{2,1,0:T(8,128)(2,1)S(1)}, u32[]{:S(2)}, u32[]{:S(2)}) collective-permute-start(bf16[2,192,1024]{2,1,0:T(8,128)(2,1)S(1)} %fusion.59), channel_id=1, source_target_pairs={{0,8},{1,33},{4,12},{5,37},{8,0},{9,41},{12,4},{13,45},{16,24},{17... | collective-permute-start | bytes 2359304 | tf_op jit(solution)/shard_map/ppermute | solution.py:26
  49.2 4.5 %collective-permute-done.8 = bf16[2,192,1024]{2,1,0:T(8,128)(2,1)S(1)} collective-permute-done((bf16[2,192,1024]{2,1,0:T(8,128)(2,1)S(1)}, bf16[2,192,1024]{2,1,0:T(8,128)(2,1)S(1)}, u32[]{:S(2)}, u32[]{:S(2)}) %collective-permute-start.8) | collective-permute-done | bytes 786464 | tf_op jit(solution)/shard_map/ppermute | solution.py:26
  53.7 8.2 %collective-permute-done.7 = bf16[2,192,1024]{2,1,0:T(8,128)(2,1)S(1)} collective-permute-done((bf16[2,192,1024]{2,1,0:T(8,128)(2,1)S(1)}, bf16[2,192,1024]{2,1,0:T(8,128)(2,1)S(1)}, u32[]{:S(2)}, u32[]{:S(2)}) %collective-permute-start.7) | collective-permute-done | bytes 786464 | tf_op jit(solution)/shard_map/ppermute | solution.py:26
  72.9 3.3 %collective-permute-start.19 = (bf16[256,768]{1,0:T(8,128)(2,1)S(1)}, bf16[256,768]{1,0:T(8,128)(2,1)S(1)}, u32[]{:S(2)}, u32[]{:S(2)}) collective-permute-start(bf16[256,768]{1,0:T(8,128)(2,1)S(1)} %get-tuple-element.42), channel_id=1, source_target_pairs={{0,48},{1,13},{4,52},{5,1},{8,56},{9,5},{12,60},{13,9},{16,0},{17,... | collective-permute-start | bytes 1179656 | tf_op jit(solution)/shard_map/ppermute | solution.py:30
  78.5 3.4 %collective-permute-start.12 = (bf16[2,256,768]{2,1,0:T(8,128)(2,1)S(1)}, bf16[2,256,768]{2,1,0:T(8,128)(2,1)S(1)}, u32[]{:S(2)}, u32[]{:S(2)}) collective-permute-start(bf16[2,256,768]{2,1,0:T(8,128)(2,1)S(1)} %pad_maximum_fusion.11), channel_id=1, source_target_pairs={{0,48},{1,13},{4,52},{5,1},{8,56},{9,5},{12,60},{13,9},{16,0},{17,... | collective-permute-start | bytes 2359304 | tf_op jit(solution)/shard_map/ppermute | solution.py:30
  82.7 3.4 %collective-permute-start.20 = (bf16[2,256,768]{2,1,0:T(8,128)(2,1)S(1)}, bf16[2,256,768]{2,1,0:T(8,128)(2,1)S(1)}, u32[]{:S(2)}, u32[]{:S(2)}) collective-permute-start(bf16[2,256,768]{2,1,0:T(8,128)(2,1)S(1)} %pad_maximum_fusion.15), channel_id=1, source_target_pairs={{0,48},{1,13},{4,52},{5,1},{8,56},{9,5},{12,60},{13,9},{16,0},{17,... | collective-permute-start | bytes 2359304 | tf_op jit(solution)/shard_map/ppermute | solution.py:30
  86.4 5.0 %collective-permute-done.12 = bf16[2,256,768]{2,1,0:T(8,128)(2,1)S(1)} collective-permute-done((bf16[2,256,768]{2,1,0:T(8,128)(2,1)S(1)}, bf16[2,256,768]{2,1,0:T(8,128)(2,1)S(1)}, u32[]{:S(2)}, u32[]{:S(2)}) %collective-permute-start.12) | collective-permute-done | bytes 786464 | tf_op jit(solution)/shard_map/ppermute | solution.py:30
  91.4 4.3 %collective-permute-done.10 = bf16[2,256,768]{2,1,0:T(8,128)(2,1)S(1)} collective-permute-done((bf16[2,256,768]{2,1,0:T(8,128)(2,1)S(1)}, bf16[2,256,768]{2,1,0:T(8,128)(2,1)S(1)}, u32[]{:S(2)}, u32[]{:S(2)}) %collective-permute-start.10) | collective-permute-done | bytes 786464 | tf_op jit(solution)/shard_map/ppermute | solution.py:30
  99.8 4.3 %collective-permute-done.18 = bf16[2,256,768]{2,1,0:T(8,128)(2,1)S(1)} collective-permute-done((bf16[2,256,768]{2,1,0:T(8,128)(2,1)S(1)}, bf16[2,256,768]{2,1,0:T(8,128)(2,1)S(1)}, u32[]{:S(2)}, u32[]{:S(2)}) %collective-permute-start.18) | collective-permute-done | bytes 786464 | tf_op jit(solution)/shard_map/ppermute | solution.py:30
  105.7 13.6 %collective-permute-done.13 = bf16[2,256,768]{2,1,0:T(8,128)(2,1)} collective-permute-done((bf16[2,256,768]{2,1,0:T(8,128)(2,1)}, bf16[2,256,768]{2,1,0:T(8,128)(2,1)}, u32[]{:S(2)}, u32[]{:S(2)}) %collective-permute-start.13) | collective-permute-done | bytes 786464 | tf_op jit(solution)/shard_map/ppermute | solution.py:34
  121.7 3.2 %collective-permute-start.14 = (bf16[2,256,768]{2,1,0:T(8,128)(2,1)S(1)}, bf16[2,256,768]{2,1,0:T(8,128)(2,1)S(1)}, u32[]{:S(2)}, u32[]{:S(2)}) collective-permute-start(bf16[2,256,768]{2,1,0:T(8,128)(2,1)S(1)} %pad_maximum_fusion.12), channel_id=1, source_target_pairs={{0,48},{1,13},{4,52},{5,1},{8,56},{9,5},{12,60},{13,9},{16,0},{17,... | collective-permute-start | bytes 2359304 | tf_op jit(solution)/shard_map/ppermute | solution.py:30
  125.0 6.8 %collective-permute-done.21 = bf16[2,256,768]{2,1,0:T(8,128)(2,1)} collective-permute-done((bf16[2,256,768]{2,1,0:T(8,128)(2,1)}, bf16[2,256,768]{2,1,0:T(8,128)(2,1)}, u32[]{:S(2)}, u32[]{:S(2)}) %collective-permute-start.21) | collective-permute-done | bytes 786464 | tf_op jit(solution)/shard_map/ppermute | solution.py:34
  138.7 3.3 %collective-permute-start.31 = (bf16[256,768]{1,0:T(8,128)(2,1)S(1)}, bf16[256,768]{1,0:T(8,128)(2,1)S(1)}, u32[]{:S(2)}, u32[]{:S(2)}) collective-permute-start(bf16[256,768]{1,0:T(8,128)(2,1)S(1)} %get-tuple-element.74), channel_id=1, source_target_pairs={{0,48},{1,13},{4,52},{5,1},{8,56},{9,5},{12,60},{13,9},{16,0},{17,... | collective-permute-start | bytes 1179656 | tf_op jit(solution)/shard_map/ppermute | solution.py:30
  142.0 5.2 %collective-permute-done.23 = bf16[2,256,768]{2,1,0:T(8,128)(2,1)S(1)} collective-permute-done((bf16[2,256,768]{2,1,0:T(8,128)(2,1)S(1)}, bf16[2,256,768]{2,1,0:T(8,128)(2,1)S(1)}, u32[]{:S(2)}, u32[]{:S(2)}) %collective-permute-start.23) | collective-permute-done | bytes 786464 | tf_op jit(solution)/shard_map/ppermute | solution.py:30
  147.4 4.0 %collective-permute-start.32 = (bf16[256,768]{1,0:T(8,128)(2,1)S(1)}, bf16[256,768]{1,0:T(8,128)(2,1)S(1)}, u32[]{:S(2)}, u32[]{:S(2)}) collective-permute-start(bf16[256,768]{1,0:T(8,128)(2,1)S(1)} %get-tuple-element.78), channel_id=1, source_target_pairs={{0,48},{1,13},{4,52},{5,1},{8,56},{9,5},{12,60},{13,9},{16,0},{17,... | collective-permute-start | bytes 1179656 | tf_op jit(solution)/shard_map/ppermute | solution.py:30
  173.6 4.1 %collective-permute-done.26 = bf16[192,1024]{1,0:T(8,128)(2,1)S(1)} collective-permute-done((bf16[192,1024]{1,0:T(8,128)(2,1)S(1)}, bf16[192,1024]{1,0:T(8,128)(2,1)S(1)}, u32[]{:S(2)}, u32[]{:S(2)}) %collective-permute-start.26) | collective-permute-done | bytes 393248 | tf_op jit(solution)/shard_map/ppermute | solution.py:26
  180.8 4.1 %collective-permute-done.29 = bf16[192,256]{1,0:T(8,128)(2,1)S(1)} collective-permute-done((bf16[192,256]{1,0:T(8,128)(2,1)S(1)}, bf16[192,256]{1,0:T(8,128)(2,1)S(1)}, u32[]{:S(2)}, u32[]{:S(2)}) %collective-permute-start.29) | collective-permute-done | bytes 98336 | tf_op jit(solution)/shard_map/ppermute | solution.py:34
  187.0 4.2 %collective-permute-done.30 = bf16[192,128]{1,0:T(8,128)(2,1)S(1)} collective-permute-done((bf16[192,128]{1,0:T(8,128)(2,1)S(1)}, bf16[192,128]{1,0:T(8,128)(2,1)S(1)}, u32[]{:S(2)}, u32[]{:S(2)}) %collective-permute-start.30) | collective-permute-done | bytes 49184 | tf_op jit(solution)/shard_map/ppermute | solution.py:34
  193.5 2.9 %convert_dynamic-update-slice_fusion.2 = (f32[192,6144]{1,0:T(8,128)}, f32[192,6144]{1,0:T(8,128)}) fusion(f32[192,6144]{1,0:T(8,128)} %get-tuple-element.50, s32[]{:T(128)S(6)} %select_n.111, bf16[384,1536]{1,0:T(8,128)(2,1)} %collective-permute-done.33, f32[192,6144]{1,0:T(8,128)} %get-tuple-element.51), kind=kLoop, calls=%fused_computation.52 | loop fusion | flops 589824 | bytes 3538948 | tf_op jit(solution)/shard_map/dynamic_update_slice | solution.py:153
  199.4 3.7 %collective-permute-done.35 = bf16[384,1536]{1,0:T(8,128)(2,1)} collective-permute-done((bf16[384,1536]{1,0:T(8,128)(2,1)S(1)}, bf16[384,1536]{1,0:T(8,128)(2,1)}, u32[]{:S(2)}, u32[]{:S(2)}) %collective-permute-start.35) | collective-permute-done | bytes 1179680 | tf_op jit(solution)/shard_map/ppermute | solution.py:26
  (167 shorter events, 85.2 us)
Async XLA Ops:
  2.7 13.9 %collective-permute-start = (bf16[2,192,128]{2,1,0:T(8,128)(2,1)S(1)}, bf16[2,192,128]{2,1,0:T(8,128)(2,1)S(1)}, u32[]{:S(2)}, u32[]{:S(2)}) collective-permute-start(bf16[2,192,128]{2,1,0:T(8,128)(2,1)S(1)} %get-tuple-element.91), channel_id=1, source_target_pairs={{0,64},{64,0},{1,65},{65,1},{2,66},{66,2},{3,67},{67,3},{4,68},{68... | collective-permute-start | bytes 294920 | tf_op jit(solution)/shard_map/ppermute | solution.py:34
  9.3 18.0 %collective-permute-start.5 = (bf16[384,1536]{1,0:T(8,128)(2,1)}, bf16[384,1536]{1,0:T(8,128)(2,1)S(1)}, u32[]{:S(2)}, u32[]{:S(2)}) collective-permute-start(bf16[384,1536]{1,0:T(8,128)(2,1)} %pad_maximum_fusion.8), channel_id=1, source_target_pairs={{0,8},{1,33},{4,12},{5,37},{8,0},{9,41},{12,4},{13,45},{16,24},{17... | collective-permute-start | bytes 3538952 | tf_op jit(solution)/shard_map/ppermute | solution.py:26
  13.5 26.6 %collective-permute-start.4 = (bf16[384,1536]{1,0:T(8,128)(2,1)}, bf16[384,1536]{1,0:T(8,128)(2,1)S(1)}, u32[]{:S(2)}, u32[]{:S(2)}) collective-permute-start(bf16[384,1536]{1,0:T(8,128)(2,1)} %pad_maximum_fusion.7), channel_id=1, source_target_pairs={{0,12},{1,49},{4,0},{5,53},{8,4},{9,57},{12,8},{13,61},{16,28},{17... | collective-permute-start | bytes 3538952 | tf_op jit(solution)/shard_map/ppermute | solution.py:26
  15.7 24.3 %collective-permute-start.3 = (bf16[384,1536]{1,0:T(8,128)(2,1)}, bf16[384,1536]{1,0:T(8,128)(2,1)}, u32[]{:S(2)}, u32[]{:S(2)}) collective-permute-start(bf16[384,1536]{1,0:T(8,128)(2,1)} %pad_maximum_fusion.6), channel_id=1, source_target_pairs={{0,4},{1,17},{4,8},{5,21},{8,12},{9,25},{12,0},{13,29},{16,20},{17... | collective-permute-start | bytes 3538952 | tf_op jit(solution)/shard_map/ppermute | solution.py:26
  40.0 13.6 %collective-permute-start.8 = (bf16[2,192,1024]{2,1,0:T(8,128)(2,1)S(1)}, bf16[2,192,1024]{2,1,0:T(8,128)(2,1)S(1)}, u32[]{:S(2)}, u32[]{:S(2)}) collective-permute-start(bf16[2,192,1024]{2,1,0:T(8,128)(2,1)S(1)} %fusion.59), channel_id=1, source_target_pairs={{0,8},{1,33},{4,12},{5,37},{8,0},{9,41},{12,4},{13,45},{16,24},{17... | collective-permute-start | bytes 2359304 | tf_op jit(solution)/shard_map/ppermute | solution.py:26
  43.0 18.9 %collective-permute-start.7 = (bf16[2,192,1024]{2,1,0:T(8,128)(2,1)S(1)}, bf16[2,192,1024]{2,1,0:T(8,128)(2,1)S(1)}, u32[]{:S(2)}, u32[]{:S(2)}) collective-permute-start(bf16[2,192,1024]{2,1,0:T(8,128)(2,1)S(1)} %fusion.59), channel_id=1, source_target_pairs={{0,12},{1,49},{4,0},{5,53},{8,4},{9,57},{12,8},{13,61},{16,28},{17... | collective-permute-start | bytes 2359304 | tf_op jit(solution)/shard_map/ppermute | solution.py:26
  44.2 17.8 %collective-permute-start.6 = (bf16[2,192,1024]{2,1,0:T(8,128)(2,1)S(1)}, bf16[2,192,1024]{2,1,0:T(8,128)(2,1)S(1)}, u32[]{:S(2)}, u32[]{:S(2)}) collective-permute-start(bf16[2,192,1024]{2,1,0:T(8,128)(2,1)S(1)} %fusion.59), channel_id=1, source_target_pairs={{0,4},{1,17},{4,8},{5,21},{8,12},{9,25},{12,0},{13,29},{16,20},{17... | collective-permute-start | bytes 2359304 | tf_op jit(solution)/shard_map/ppermute | solution.py:26
  68.2 17.9 %collective-permute-start.17 = (bf16[256,768]{1,0:T(8,128)(2,1)S(1)}, bf16[256,768]{1,0:T(8,128)(2,1)S(1)}, u32[]{:S(2)}, u32[]{:S(2)}) collective-permute-start(bf16[256,768]{1,0:T(8,128)(2,1)S(1)} %get-tuple-element.40), channel_id=1, source_target_pairs={{0,16},{1,5},{4,20},{5,9},{8,24},{9,13},{12,28},{13,1},{16,32},{17... | collective-permute-start | bytes 1179656 | tf_op jit(solution)/shard_map/ppermute | solution.py:30
  78.5 12.9 %collective-permute-start.12 = (bf16[2,256,768]{2,1,0:T(8,128)(2,1)S(1)}, bf16[2,256,768]{2,1,0:T(8,128)(2,1)S(1)}, u32[]{:S(2)}, u32[]{:S(2)}) collective-permute-start(bf16[2,256,768]{2,1,0:T(8,128)(2,1)S(1)} %pad_maximum_fusion.11), channel_id=1, source_target_pairs={{0,48},{1,13},{4,52},{5,1},{8,56},{9,5},{12,60},{13,9},{16,0},{17,... | collective-permute-start | bytes 2359304 | tf_op jit(solution)/shard_map/ppermute | solution.py:30
  82.4 13.3 %collective-permute-start.10 = (bf16[2,256,768]{2,1,0:T(8,128)(2,1)S(1)}, bf16[2,256,768]{2,1,0:T(8,128)(2,1)S(1)}, u32[]{:S(2)}, u32[]{:S(2)}) collective-permute-start(bf16[2,256,768]{2,1,0:T(8,128)(2,1)S(1)} %pad_maximum_fusion.10), channel_id=1, source_target_pairs={{0,16},{1,5},{4,20},{5,9},{8,24},{9,13},{12,28},{13,1},{16,32},{17... | collective-permute-start | bytes 2359304 | tf_op jit(solution)/shard_map/ppermute | solution.py:30
  82.7 17.1 %collective-permute-start.20 = (bf16[2,256,768]{2,1,0:T(8,128)(2,1)S(1)}, bf16[2,256,768]{2,1,0:T(8,128)(2,1)S(1)}, u32[]{:S(2)}, u32[]{:S(2)}) collective-permute-start(bf16[2,256,768]{2,1,0:T(8,128)(2,1)S(1)} %pad_maximum_fusion.15), channel_id=1, source_target_pairs={{0,48},{1,13},{4,52},{5,1},{8,56},{9,5},{12,60},{13,9},{16,0},{17,... | collective-permute-start | bytes 2359304 | tf_op jit(solution)/shard_map/ppermute | solution.py:30
  86.3 17.9 %collective-permute-start.18 = (bf16[2,256,768]{2,1,0:T(8,128)(2,1)S(1)}, bf16[2,256,768]{2,1,0:T(8,128)(2,1)S(1)}, u32[]{:S(2)}, u32[]{:S(2)}) collective-permute-start(bf16[2,256,768]{2,1,0:T(8,128)(2,1)S(1)} %pad_maximum_fusion.14), channel_id=1, source_target_pairs={{0,16},{1,5},{4,20},{5,9},{8,24},{9,13},{12,28},{13,1},{16,32},{17... | collective-permute-start | bytes 2359304 | tf_op jit(solution)/shard_map/ppermute | solution.py:30
  97.0 22.3 %collective-permute-start.13 = (bf16[2,256,768]{2,1,0:T(8,128)(2,1)}, bf16[2,256,768]{2,1,0:T(8,128)(2,1)}, u32[]{:S(2)}, u32[]{:S(2)}) collective-permute-start(bf16[2,256,768]{2,1,0:T(8,128)(2,1)} %fusion.29), channel_id=1, source_target_pairs={{0,64},{64,0},{1,65},{65,1},{2,66},{66,2},{3,67},{67,3},{4,68},{68... | collective-permute-start | bytes 2359304 | tf_op jit(solution)/shard_map/ppermute | solution.py:34
  105.3 26.4 %collective-permute-start.21 = (bf16[2,256,768]{2,1,0:T(8,128)(2,1)}, bf16[2,256,768]{2,1,0:T(8,128)(2,1)}, u32[]{:S(2)}, u32[]{:S(2)}) collective-permute-start(bf16[2,256,768]{2,1,0:T(8,128)(2,1)} %fusion.30), channel_id=1, source_target_pairs={{0,64},{64,0},{1,65},{65,1},{2,66},{66,2},{3,67},{67,3},{4,68},{68... | collective-permute-start | bytes 2359304 | tf_op jit(solution)/shard_map/ppermute | solution.py:34
  121.7 16.8 %collective-permute-start.15 = (bf16[2,256,768]{2,1,0:T(8,128)(2,1)S(1)}, bf16[2,256,768]{2,1,0:T(8,128)(2,1)S(1)}, u32[]{:S(2)}, u32[]{:S(2)}) collective-permute-start(bf16[2,256,768]{2,1,0:T(8,128)(2,1)S(1)} %pad_maximum_fusion.12), channel_id=1, source_target_pairs={{0,16},{1,5},{4,20},{5,9},{8,24},{9,13},{12,28},{13,1},{16,32},{17... | collective-permute-start | bytes 2359304 | tf_op jit(solution)/shard_map/ppermute | solution.py:30
  121.7 16.9 %collective-permute-start.14 = (bf16[2,256,768]{2,1,0:T(8,128)(2,1)S(1)}, bf16[2,256,768]{2,1,0:T(8,128)(2,1)S(1)}, u32[]{:S(2)}, u32[]{:S(2)}) collective-permute-start(bf16[2,256,768]{2,1,0:T(8,128)(2,1)S(1)} %pad_maximum_fusion.12), channel_id=1, source_target_pairs={{0,48},{1,13},{4,52},{5,1},{8,56},{9,5},{12,60},{13,9},{16,0},{17,... | collective-permute-start | bytes 2359304 | tf_op jit(solution)/shard_map/ppermute | solution.py:30
  133.9 13.3 %collective-permute-start.23 = (bf16[2,256,768]{2,1,0:T(8,128)(2,1)S(1)}, bf16[2,256,768]{2,1,0:T(8,128)(2,1)S(1)}, u32[]{:S(2)}, u32[]{:S(2)}) collective-permute-start(bf16[2,256,768]{2,1,0:T(8,128)(2,1)S(1)} %pad_maximum_fusion.16), channel_id=1, source_target_pairs={{0,16},{1,5},{4,20},{5,9},{8,24},{9,13},{12,28},{13,1},{16,32},{17... | collective-permute-start | bytes 2359304 | tf_op jit(solution)/shard_map/ppermute | solution.py:30
  135.0 12.4 %collective-permute-start.22 = (bf16[2,256,768]{2,1,0:T(8,128)(2,1)S(1)}, bf16[2,256,768]{2,1,0:T(8,128)(2,1)S(1)}, u32[]{:S(2)}, u32[]{:S(2)}) collective-permute-start(bf16[2,256,768]{2,1,0:T(8,128)(2,1)S(1)} %pad_maximum_fusion.16), channel_id=1, source_target_pairs={{0,48},{1,13},{4,52},{5,1},{8,56},{9,5},{12,60},{13,9},{16,0},{17,... | collective-permute-start | bytes 2359304 | tf_op jit(solution)/shard_map/ppermute | solution.py:30
  138.5 14.6 %collective-permute-start.16 = (bf16[256,768]{1,0:T(8,128)(2,1)S(1)}, bf16[256,768]{1,0:T(8,128)(2,1)S(1)}, u32[]{:S(2)}, u32[]{:S(2)}) collective-permute-start(bf16[256,768]{1,0:T(8,128)(2,1)S(1)} %get-tuple-element.77), channel_id=1, source_target_pairs={{0,16},{1,5},{4,20},{5,9},{8,24},{9,13},{12,28},{13,1},{16,32},{17... | collective-permute-start | bytes 1179656 | tf_op jit(solution)/shard_map/ppermute | solution.py:30
  138.7 12.9 %collective-permute-start.31 = (bf16[256,768]{1,0:T(8,128)(2,1)S(1)}, bf16[256,768]{1,0:T(8,128)(2,1)S(1)}, u32[]{:S(2)}, u32[]{:S(2)}) collective-permute-start(bf16[256,768]{1,0:T(8,128)(2,1)S(1)} %get-tuple-element.74), channel_id=1, source_target_pairs={{0,48},{1,13},{4,52},{5,1},{8,56},{9,5},{12,60},{13,9},{16,0},{17,... | collective-permute-start | bytes 1179656 | tf_op jit(solution)/shard_map/ppermute | solution.py:30
  165.1 12.6 %collective-permute-start.26 = (bf16[192,1024]{1,0:T(8,128)(2,1)S(1)}, bf16[192,1024]{1,0:T(8,128)(2,1)S(1)}, u32[]{:S(2)}, u32[]{:S(2)}) collective-permute-start(bf16[192,1024]{1,0:T(8,128)(2,1)S(1)} %get-tuple-element.27), channel_id=1, source_target_pairs={{0,4},{1,17},{4,8},{5,21},{8,12},{9,25},{12,0},{13,29},{16,20},{17... | collective-permute-start | bytes 1179656 | tf_op jit(solution)/shard_map/ppermute | solution.py:26
  166.1 27.4 %collective-permute-start.33 = (bf16[384,1536]{1,0:T(8,128)(2,1)S(1)}, bf16[384,1536]{1,0:T(8,128)(2,1)}, u32[]{:S(2)}, u32[]{:S(2)}) collective-permute-start(bf16[384,1536]{1,0:T(8,128)(2,1)S(1)} %maximum_maximum_fusion.1), channel_id=1, source_target_pairs={{0,12},{1,49},{4,0},{5,53},{8,4},{9,57},{12,8},{13,61},{16,28},{17... | collective-permute-start | bytes 3538952 | tf_op jit(solution)/shard_map/ppermute | solution.py:26
  168.9 27.6 %collective-permute-start.34 = (bf16[384,1536]{1,0:T(8,128)(2,1)S(1)}, bf16[384,1536]{1,0:T(8,128)(2,1)}, u32[]{:S(2)}, u32[]{:S(2)}) collective-permute-start(bf16[384,1536]{1,0:T(8,128)(2,1)S(1)} %maximum_maximum_fusion.2), channel_id=1, source_target_pairs={{0,4},{1,17},{4,8},{5,21},{8,12},{9,25},{12,0},{13,29},{16,20},{17... | collective-permute-start | bytes 3538952 | tf_op jit(solution)/shard_map/ppermute | solution.py:26
  178.3 24.8 %collective-permute-start.35 = (bf16[384,1536]{1,0:T(8,128)(2,1)S(1)}, bf16[384,1536]{1,0:T(8,128)(2,1)}, u32[]{:S(2)}, u32[]{:S(2)}) collective-permute-start(bf16[384,1536]{1,0:T(8,128)(2,1)S(1)} %maximum_maximum_fusion.3), channel_id=1, source_target_pairs={{0,8},{1,33},{4,12},{5,37},{8,0},{9,41},{12,4},{13,45},{16,24},{17... | collective-permute-start | bytes 3538952 | tf_op jit(solution)/shard_map/ppermute | solution.py:26
  (31 other events, 207.2 us)
